TPU v7x, 32 devices: a whole 2x2x4 slice. The times are simulated.
32 devices in a mesh: rep: 4 (over x, core), shard: 8 (over z, y).
Axes of the slice: x: 2, y: 2, z: 4, core: 2. Of those that a mesh axis runs over, the one named last changes fastest.
Arguments:
- tokens: bfloat16 [16384, 1024], P(('rep', 'shard')), may hold values from -6 to 6
- cotangent: bfloat16 [16384, 1024], P(('rep', 'shard')), may hold values from -6 to 6
- attn_gain: bfloat16 [1024], P('shard'), may hold values from 0.5 to 1.5
- query_gain: bfloat16 [128], P('shard'), may hold values from 0.25 to 1.75
- key_gain: bfloat16 [128], P('shard'), may hold values from 0.25 to 1.75
- query_proj: bfloat16 [1024, 2048], P('shard'), may hold values from -0.1875 to 0.1875
- key_proj: bfloat16 [1024, 1024], P('shard'), may hold values from -0.1875 to 0.1875
- value_proj: bfloat16 [1024, 1024], P('shard'), may hold values from -0.1875 to 0.1875
- out_proj: bfloat16 [2048, 1024], P('shard'), may hold values from -0.75 to 0.75
- mlp_gain: bfloat16 [1024], P('shard'), may hold values from 0.5 to 1.5
- gate_proj: bfloat16 [1024, 3072], P('shard'), may hold values from -0.1875 to 0.1875
- up_proj: bfloat16 [1024, 3072], P('shard'), may hold values from -0.1875 to 0.1875
- down_proj: bfloat16 [3072, 1024], P('shard'), may hold values from -0.109375 to 0.109375
Outputs:
- layer_out: bfloat16 [16384, 1024], P(('rep', 'shard'))
- tokens_grad: float32 [16384, 1024], P(('rep', 'shard'))
- attn_gain_grad: float32 [1024], P('shard')
- query_gain_grad: float32 [128], P('shard')
- key_gain_grad: float32 [128], P('shard')
- query_proj_grad: float32 [1024, 2048], P('shard')
- key_proj_grad: float32 [1024, 1024], P('shard')
- value_proj_grad: float32 [1024, 1024], P('shard')
- out_proj_grad: float32 [2048, 1024], P('shard')
- mlp_gain_grad: float32 [1024], P('shard')
- gate_proj_grad: float32 [1024, 3072], P('shard')
- up_proj_grad: float32 [1024, 3072], P('shard')
- down_proj_grad: float32 [3072, 1024], P('shard')
All inputs are finite; a program needn't handle non-finite values.
Results may differ from a plain program's by a relative error of at most 0.02.
Values may be sent and summed in bfloat16 or wider, within the bound.
A program may use at most 192 MiB of HBM per device.

v0:
```python
import jax
import jax.numpy as jnp
from jax import lax
from jax.sharding import PartitionSpec as P

EPS = 1e-06
THETA = 1000000.0


def product(left, right):
    return jnp.dot(left, right, preferred_element_type=jnp.float32)


def left_product(left, right):
    return lax.dot_general(
        left, right, (((0,), (0,)), ((), ())), preferred_element_type=jnp.float32
    )


def right_product(left, right):
    return lax.dot_general(
        left, right, (((1,), (1,)), ((), ())), preferred_element_type=jnp.float32
    )


def rotary_tables(length, width):
    half_width = width // 2
    frequency = THETA ** (-(jnp.arange(half_width, dtype=jnp.float32) * 2.0) / width)
    angles = jnp.arange(length, dtype=jnp.float32)[:, None] * frequency[None, :]
    angles = jnp.concatenate([angles, angles], axis=1)
    return (jnp.cos(angles)[:, None, :], jnp.sin(angles)[:, None, :])


def rotate(values):
    half_width = values.shape[-1] // 2
    return jnp.concatenate([-values[..., half_width:], values[..., :half_width]], axis=-1)


def rotate_back(values):
    half_width = values.shape[-1] // 2
    return jnp.concatenate([values[..., half_width:], -values[..., :half_width]], axis=-1)


def inverse_rms(values):
    return lax.rsqrt(jnp.mean(values * values, axis=-1, keepdims=True) + EPS)


def norm_back(grads, values, inverse, gain):
    weighted = grads * gain
    return inverse * weighted - values * (inverse * inverse * inverse) * jnp.mean(
        weighted * values, axis=-1, keepdims=True
    )


def masked_scores(query_b, key_b):
    head_size = query_b.shape[-1]
    length = query_b.shape[0]
    scores = jnp.einsum(
        "qgjd,kgd->gjqk", query_b, key_b, preferred_element_type=jnp.float32
    ) * head_size ** (-0.5)
    causal = jnp.arange(length)[:, None] >= jnp.arange(length)[None, :]
    return jnp.where(causal, scores, -1e30)


def attend(query_b, key_b, value_b):
    scores = masked_scores(query_b, key_b)
    highest = jnp.max(scores, axis=-1, keepdims=True)
    powers = jnp.exp(scores - highest)
    totals = jnp.sum(powers, axis=-1, keepdims=True)
    probs_b = (powers / totals).astype(jnp.bfloat16)
    mixed = jnp.einsum("gjqk,kgd->qgjd", probs_b, value_b, preferred_element_type=jnp.float32)
    return (mixed, highest + jnp.log(totals))


def attend_back(query_b, key_b, value_b, log_totals, grad_mixed):
    head_size = query_b.shape[-1]
    probs = jnp.exp(masked_scores(query_b, key_b) - log_totals)
    probs_b = probs.astype(jnp.bfloat16)
    grad_probs = jnp.einsum(
        "qgjd,kgd->gjqk", grad_mixed, value_b, preferred_element_type=jnp.float32
    )
    value_grad = jnp.einsum(
        "gjqk,qgjd->kgd", probs_b, grad_mixed, preferred_element_type=jnp.float32
    )
    grad_scores = probs * (grad_probs - jnp.sum(probs * grad_probs, axis=-1, keepdims=True))
    grad_scores = grad_scores.astype(jnp.bfloat16)
    grad_qrot = jnp.einsum(
        "gjqk,kgd->qgjd", grad_scores, key_b, preferred_element_type=jnp.float32
    ) * head_size ** (-0.5)
    grad_krot = jnp.einsum(
        "gjqk,qgjd->kgd", grad_scores, query_b, preferred_element_type=jnp.float32
    ) * head_size ** (-0.5)
    return (grad_qrot, grad_krot, value_grad)


def shards(
    tokens,
    cotangent,
    attn_gain,
    query_gain,
    key_gain,
    query_proj,
    key_proj,
    value_proj,
    out_proj,
    mlp_gain,
    gate_proj,
    up_proj,
    down_proj,
):
    attn_full = (
        lax.all_gather(attn_gain, "shard", axis=0, tiled=True),
        lax.all_gather(query_gain, "shard", axis=0, tiled=True),
        lax.all_gather(key_gain, "shard", axis=0, tiled=True),
        lax.all_gather(query_proj, "shard", axis=0, tiled=True),
        lax.all_gather(key_proj, "shard", axis=0, tiled=True),
        lax.all_gather(value_proj, "shard", axis=0, tiled=True),
        lax.all_gather(out_proj, "shard", axis=0, tiled=True),
    )
    attn_scale = attn_full[0].astype(jnp.float32)
    query_scale = attn_full[1].astype(jnp.float32)
    key_scale = attn_full[2].astype(jnp.float32)
    query_full, key_full, value_full, out_full = (
        attn_full[3],
        attn_full[4],
        attn_full[5],
        attn_full[6],
    )
    head_size = query_scale.shape[0]
    query_heads = query_full.shape[1] // head_size
    key_heads = key_full.shape[1] // head_size
    group_size = query_heads // key_heads
    inputs = tokens.astype(jnp.float32)
    length = inputs.shape[0]
    cosine, sine = rotary_tables(length, head_size)
    inv_one = inverse_rms(inputs)
    normed = (inputs * inv_one * attn_scale).astype(jnp.bfloat16)
    query_raw = product(normed, query_full).reshape(length, query_heads, head_size)
    key_raw = product(normed, key_full).reshape(length, key_heads, head_size)
    value_b = product(normed, value_full).astype(jnp.bfloat16).reshape(length, key_heads, head_size)
    inv_query = inverse_rms(query_raw)
    inv_key = inverse_rms(key_raw)
    query_normed = query_raw * inv_query * query_scale
    key_normed = key_raw * inv_key * key_scale
    query_rot = (
        (query_normed * cosine + rotate(query_normed) * sine)
        .astype(jnp.bfloat16)
        .reshape(length, key_heads, group_size, head_size)
    )
    key_rot = (key_normed * cosine + rotate(key_normed) * sine).astype(jnp.bfloat16)
    mixed, log_totals = attend(query_rot, key_rot, value_b)
    mixed_b = mixed.reshape(length, query_heads * head_size).astype(jnp.bfloat16)
    middle = inputs + product(mixed_b, out_full)
    mlp_full = (
        lax.all_gather(mlp_gain, "shard", axis=0, tiled=True),
        lax.all_gather(gate_proj, "shard", axis=0, tiled=True),
        lax.all_gather(up_proj, "shard", axis=0, tiled=True),
        lax.all_gather(down_proj, "shard", axis=0, tiled=True),
    )
    mlp_scale = mlp_full[0].astype(jnp.float32)
    inv_two = inverse_rms(middle)
    inner = (middle * inv_two * mlp_scale).astype(jnp.bfloat16)
    gate_value = product(inner, mlp_full[1])
    up_value = product(inner, mlp_full[2])
    silu_gate = jax.nn.silu(gate_value)
    hidden = (silu_gate * up_value).astype(jnp.bfloat16)
    layer_out = (middle + product(hidden, mlp_full[3])).astype(jnp.bfloat16)
    mlp_back = (
        lax.all_gather(mlp_gain, "shard", axis=0, tiled=True),
        lax.all_gather(gate_proj, "shard", axis=0, tiled=True),
        lax.all_gather(up_proj, "shard", axis=0, tiled=True),
        lax.all_gather(down_proj, "shard", axis=0, tiled=True),
    )
    down_grad = left_product(hidden, cotangent)
    grad_hidden = right_product(cotangent, mlp_back[3])
    sigmoid_gate = jax.nn.sigmoid(gate_value)
    grad_gate = (
        grad_hidden * up_value * (sigmoid_gate + gate_value * sigmoid_gate * (1.0 - sigmoid_gate))
    ).astype(jnp.bfloat16)
    grad_up = (grad_hidden * silu_gate).astype(jnp.bfloat16)
    gate_grad = left_product(inner, grad_gate)
    up_grad = left_product(inner, grad_up)
    grad_inner = right_product(grad_gate, mlp_back[1]) + right_product(grad_up, mlp_back[2])
    mlp_gain_grad = jnp.sum(grad_inner * middle * inv_two, axis=0)
    grad_middle = cotangent.astype(jnp.float32) + norm_back(
        grad_inner, middle, inv_two, mlp_back[0].astype(jnp.float32)
    )
    mlp_shards = (
        lax.psum_scatter(
            mlp_gain_grad.astype(jnp.bfloat16), "shard", scatter_dimension=0, tiled=True
        ).astype(jnp.float32),
        lax.psum_scatter(
            gate_grad.astype(jnp.bfloat16), "shard", scatter_dimension=0, tiled=True
        ).astype(jnp.float32),
        lax.psum_scatter(
            up_grad.astype(jnp.bfloat16), "shard", scatter_dimension=0, tiled=True
        ).astype(jnp.float32),
        lax.psum_scatter(
            down_grad.astype(jnp.bfloat16), "shard", scatter_dimension=0, tiled=True
        ).astype(jnp.float32),
    )
    mlp_shards = (
        lax.psum(mlp_shards[0].astype(jnp.bfloat16), "rep").astype(jnp.float32),
        lax.psum(mlp_shards[1].astype(jnp.bfloat16), "rep").astype(jnp.float32),
        lax.psum(mlp_shards[2].astype(jnp.bfloat16), "rep").astype(jnp.float32),
        lax.psum(mlp_shards[3].astype(jnp.bfloat16), "rep").astype(jnp.float32),
    )
    attn_back = (
        lax.all_gather(attn_gain, "shard", axis=0, tiled=True),
        lax.all_gather(query_gain, "shard", axis=0, tiled=True),
        lax.all_gather(key_gain, "shard", axis=0, tiled=True),
        lax.all_gather(query_proj, "shard", axis=0, tiled=True),
        lax.all_gather(key_proj, "shard", axis=0, tiled=True),
        lax.all_gather(value_proj, "shard", axis=0, tiled=True),
        lax.all_gather(out_proj, "shard", axis=0, tiled=True),
    )
    grad_attn = grad_middle.astype(jnp.bfloat16)
    out_grad = left_product(mixed_b, grad_attn)
    grad_mixed = (
        right_product(grad_attn, attn_back[6])
        .astype(jnp.bfloat16)
        .reshape(length, key_heads, group_size, head_size)
    )
    grad_qrot, grad_krot, value_grad = attend_back(
        query_rot, key_rot, value_b, log_totals, grad_mixed
    )
    grad_qrot = grad_qrot.reshape(length, query_heads, head_size)
    grad_qnorm = grad_qrot * cosine + rotate_back(grad_qrot * sine)
    grad_knorm = grad_krot * cosine + rotate_back(grad_krot * sine)
    query_gain_grad = jnp.sum(grad_qnorm * query_raw * inv_query, axis=(0, 1))
    key_gain_grad = jnp.sum(grad_knorm * key_raw * inv_key, axis=(0, 1))
    grad_query = norm_back(grad_qnorm, query_raw, inv_query, attn_back[1].astype(jnp.float32))
    grad_query = grad_query.astype(jnp.bfloat16).reshape(length, query_heads * head_size)
    grad_key = norm_back(grad_knorm, key_raw, inv_key, attn_back[2].astype(jnp.float32))
    grad_key = grad_key.astype(jnp.bfloat16).reshape(length, key_heads * head_size)
    value_grad = value_grad.astype(jnp.bfloat16).reshape(length, key_heads * head_size)
    query_grad = left_product(normed, grad_query)
    key_grad = left_product(normed, grad_key)
    value_weight_grad = left_product(normed, value_grad)
    grad_normed = (
        right_product(grad_query, attn_back[3])
        + right_product(grad_key, attn_back[4])
        + right_product(value_grad, attn_back[5])
    )
    attn_gain_grad = jnp.sum(grad_normed * inputs * inv_one, axis=0)
    tokens_grad = grad_middle + norm_back(
        grad_normed, inputs, inv_one, attn_back[0].astype(jnp.float32)
    )
    attn_shards = (
        lax.psum_scatter(
            attn_gain_grad.astype(jnp.bfloat16), "shard", scatter_dimension=0, tiled=True
        ).astype(jnp.float32),
        lax.psum_scatter(
            query_gain_grad.astype(jnp.bfloat16), "shard", scatter_dimension=0, tiled=True
        ).astype(jnp.float32),
        lax.psum_scatter(
            key_gain_grad.astype(jnp.bfloat16), "shard", scatter_dimension=0, tiled=True
        ).astype(jnp.float32),
        lax.psum_scatter(
            query_grad.astype(jnp.bfloat16), "shard", scatter_dimension=0, tiled=True
        ).astype(jnp.float32),
        lax.psum_scatter(
            key_grad.astype(jnp.bfloat16), "shard", scatter_dimension=0, tiled=True
        ).astype(jnp.float32),
        lax.psum_scatter(
            value_weight_grad.astype(jnp.bfloat16), "shard", scatter_dimension=0, tiled=True
        ).astype(jnp.float32),
        lax.psum_scatter(
            out_grad.astype(jnp.bfloat16), "shard", scatter_dimension=0, tiled=True
        ).astype(jnp.float32),
    )
    attn_shards = (
        lax.psum(attn_shards[0].astype(jnp.bfloat16), "rep").astype(jnp.float32),
        lax.psum(attn_shards[1].astype(jnp.bfloat16), "rep").astype(jnp.float32),
        lax.psum(attn_shards[2].astype(jnp.bfloat16), "rep").astype(jnp.float32),
        lax.psum(attn_shards[3].astype(jnp.bfloat16), "rep").astype(jnp.float32),
        lax.psum(attn_shards[4].astype(jnp.bfloat16), "rep").astype(jnp.float32),
        lax.psum(attn_shards[5].astype(jnp.bfloat16), "rep").astype(jnp.float32),
        lax.psum(attn_shards[6].astype(jnp.bfloat16), "rep").astype(jnp.float32),
    )
    return (
        layer_out,
        tokens_grad,
        attn_shards[0],
        attn_shards[1],
        attn_shards[2],
        attn_shards[3],
        attn_shards[4],
        attn_shards[5],
        attn_shards[6],
        mlp_shards[0],
        mlp_shards[1],
        mlp_shards[2],
        mlp_shards[3],
    )


def solution(mesh):
    in_specs = (
        P(("rep", "shard"), None),
        P(("rep", "shard"), None),
        P("shard"),
        P("shard"),
        P("shard"),
        P("shard", None),
        P("shard", None),
        P("shard", None),
        P("shard", None),
        P("shard"),
        P("shard", None),
        P("shard", None),
        P("shard", None),
    )
    out_specs = (
        P(("rep", "shard"), None),
        P(("rep", "shard"), None),
        P("shard"),
        P("shard"),
        P("shard"),
        P("shard", None),
        P("shard", None),
        P("shard", None),
        P("shard", None),
        P("shard"),
        P("shard", None),
        P("shard", None),
        P("shard", None),
    )
    return jax.shard_map(shards, mesh=mesh, in_specs=in_specs, out_specs=out_specs, check_vma=False)
```

profile of v0, /device:TPU:0, one launch (start us, length us, event | category | flops | bytes accessed | tf_op | source)
XLA Modules:
  0.0 1413.8 jit_solution(9337584835907625565)
XLA Ops:
  12.8 22.2 %all-gather = bf16[8,1,128]{2,1,0:T(2,128)(2,1)S(1)} all-gather(bf16[1,1,128]{2,1,0:T(2,128)(2,1)S(1)} %bitcast.176), channel_id=1, replica_groups=mesh['rep'=4,'shard'=8] {'shard'}, dimensions={0}, use_global_device_ids=true | all-gather | bytes 2304 | tf_op jit(solution)/shard_map/all_gather | solution.py:112
  37.6 17.6 %all-reduce.7 = (bf16[128]{0:T(256)(128)(2,1)S(1)}, bf16[128]{0:T(256)(128)(2,1)S(1)}) all-reduce(bf16[128]{0:T(256)(128)(2,1)S(1)} %dynamic-update-slice, bf16[128]{0:T(256)(128)(2,1)S(1)} %dynamic-update-slice.1), channel_id=1, replica_groups=mesh['rep'=4,'shard'=8] {'shard'}, use_global_device_ids=true, to_apply=%add | all-reduce | flops 256 | bytes 1024
  57.1 18.0 %all-gather.1 = bf16[8,1,128]{2,1,0:T(2,128)(2,1)S(1)} all-gather(bf16[1,1,128]{2,1,0:T(2,128)(2,1)S(1)} %bitcast.177), channel_id=1, replica_groups=mesh['rep'=4,'shard'=8] {'shard'}, dimensions={0}, use_global_device_ids=true | all-gather | bytes 2304 | tf_op jit(solution)/shard_map/all_gather | solution.py:155
  86.3 26.4 %all-gather.10.cloned.1.call-done = bf16[1024,1024]{1,0:T(8,128)(2,1)} async-done(((bf16[128,1024]{1,0:T(8,128)(2,1)}), bf16[1024,1024]{1,0:T(8,128)(2,1)}) %all-gather.10.cloned.1.call-update) | async-done | bytes 2097168 | tf_op jit(solution)/shard_map/all_gather | solution.py:117
  119.6 67.1 %all-gather.14.cloned.1.call-done = bf16[1024,2048]{1,0:T(8,128)(2,1)} async-done(((bf16[128,2048]{1,0:T(8,128)(2,1)}), bf16[1024,2048]{1,0:T(8,128)(2,1)}) %all-gather.14.cloned.1.call-update) | async-done | bytes 4194320 | tf_op jit(solution)/shard_map/all_gather | solution.py:115
  226.0 9.2 fusion.29
  235.2 25.3 %all-gather.16.cloned.1.call-done = bf16[2048,1024]{1,0:T(8,128)(2,1)} async-done(((bf16[256,1024]{1,0:T(8,128)(2,1)}), bf16[2048,1024]{1,0:T(8,128)(2,1)}) %all-gather.16.cloned.1.call-update) | async-done | bytes 4194320 | tf_op jit(solution)/shard_map/all_gather | solution.py:118
  268.6 91.2 %all-gather.18.cloned.1.call-done = bf16[1024,3072]{1,0:T(8,128)(2,1)} async-done(((bf16[128,3072]{1,0:T(8,128)(2,1)}), bf16[1024,3072]{1,0:T(8,128)(2,1)}) %all-gather.18.cloned.1.call-update) | async-done | bytes 6291472 | tf_op jit(solution)/shard_map/all_gather | solution.py:156
  359.8 9.2 fusion.52
  369.0 90.1 %all-gather.20.cloned.1.call-done = bf16[1024,3072]{1,0:T(8,128)(2,1)} async-done(((bf16[128,3072]{1,0:T(8,128)(2,1)}), bf16[1024,3072]{1,0:T(8,128)(2,1)}) %all-gather.20.cloned.1.call-update) | async-done | bytes 6291472 | tf_op jit(solution)/shard_map/all_gather | solution.py:157
  459.1 9.3 fusion.53
  468.3 90.2 %all-gather.22.cloned.1.call-done = bf16[3072,1024]{1,0:T(8,128)(2,1)} async-done(((bf16[384,1024]{1,0:T(8,128)(2,1)}), bf16[3072,1024]{1,0:T(8,128)(2,1)}) %all-gather.22.cloned.1.call-update) | async-done | bytes 6291472 | tf_op jit(solution)/shard_map/all_gather | solution.py:158
  558.5 11.9 multiply_convert_fusion
  593.1 15.7 %fusion = (f32[8,2,512]{2,1,0:T(2,128)S(1)}, f32[8,512,512,2]{2,1,3,0:T(8,128)}) fusion(f32[8,2,512,512]{2,3,1,0:T(8,128)} %get-tuple-element.67, f32[8,2,512]{2,1,0:T(2,128)S(1)} %bitcast.160, bf16[512,8,2,128]{0,3,2,1:T(8,128)(2,1)} %bitcast.143, bf16[512,8,128,1]{2,1,0,3:T(8,128)(2,1)} %bitcast.154), kind=kOutput, calls=%fused_computation.2 | convolution fusion | flops 1086316544 | bytes 36765696 | tf_op jit(solution)/shard_map/qgjd,kgd->gjqk/dot_general | solution.py:79
  608.8 12.7 fusion.2
  689.9 10.4 multiply_reduce_fusion
  747.9 20.3 %reduce-scatter.12.cloned.1.call-done = bf16[128,1024]{1,0:T(8,128)(2,1)} async-done(((bf16[1024,1024]{1,0:T(8,128)(2,1)}), bf16[128,1024]{1,0:T(8,128)(2,1)}) %reduce-scatter.12.cloned.1.call-update) | async-done | bytes 262160 | tf_op jit(solution)/shard_map/reduce_scatter | solution.py:265
  768.2 90.5 %reduce-scatter.8.cloned.1.call-done = bf16[128,2048]{1,0:T(8,128)(2,1)} async-done(((bf16[1024,2048]{1,0:T(8,128)(2,1)}), bf16[128,2048]{1,0:T(8,128)(2,1)}) %reduce-scatter.8.cloned.1.call-update) | async-done | bytes 524304 | tf_op jit(solution)/shard_map/reduce_scatter | solution.py:259
  858.7 91.8 %reduce-scatter.14.cloned.1.call-done = bf16[256,1024]{1,0:T(8,128)(2,1)} async-done(((bf16[2048,1024]{1,0:T(8,128)(2,1)}), bf16[256,1024]{1,0:T(8,128)(2,1)}) %reduce-scatter.14.cloned.1.call-update) | async-done | bytes 524304 | tf_op jit(solution)/shard_map/reduce_scatter | solution.py:268
  950.5 121.2 %reduce-scatter.16.cloned.1.call-done = bf16[128,3072]{1,0:T(8,128)(2,1)} async-done(((bf16[1024,3072]{1,0:T(8,128)(2,1)}), bf16[128,3072]{1,0:T(8,128)(2,1)}) %reduce-scatter.16.cloned.1.call-update) | async-done | bytes 786448 | tf_op jit(solution)/shard_map/reduce_scatter | solution.py:192
  1071.6 120.7 %reduce-scatter.18.cloned.1.call-done = bf16[128,3072]{1,0:T(8,128)(2,1)} async-done(((bf16[1024,3072]{1,0:T(8,128)(2,1)}), bf16[128,3072]{1,0:T(8,128)(2,1)}) %reduce-scatter.18.cloned.1.call-update) | async-done | bytes 786448 | tf_op jit(solution)/shard_map/reduce_scatter | solution.py:195
  1192.3 120.5 %reduce-scatter.20.cloned.1.call-done = bf16[384,1024]{1,0:T(8,128)(2,1)} async-done(((bf16[3072,1024]{1,0:T(8,128)(2,1)}), bf16[384,1024]{1,0:T(8,128)(2,1)}) %reduce-scatter.20.cloned.1.call-update) | async-done | bytes 786448 | tf_op jit(solution)/shard_map/reduce_scatter | solution.py:198
  1321.1 19.8 %all-reduce.6 = (bf16[1024]{0:T(1024)(128)(2,1)S(1)}, bf16[128]{0:T(256)(128)(2,1)S(1)}, bf16[128]{0:T(256)(128)(2,1)S(1)}, bf16[1024]{0:T(1024)(128)(2,1)S(1)}) all-reduce(bf16[1024]{0:T(1024)(128)(2,1)S(1)} %get-tuple-element.17, bf16[128]{0:T(256)(128)(2,1)S(1)} %bitcast_reduce_fusion, ...), channel_id=2, replica_groups=mesh['rep'=4,'shard'=8] {'shard'}, use_global_device_ids=true, to_apply=%region_12.13.clone | all-reduce | flops 2304 | bytes 9216
  1360.9 36.3 %all-reduce.12.cloned.1.call-done = (bf16[128,2048]{1,0:T(8,128)(2,1)}, bf16[128,1024]{1,0:T(8,128)(2,1)}, bf16[128,1024]{1,0:T(8,128)(2,1)}, bf16[256,1024]{1,0...) async-done(((bf16[128,2048]{1,0:T(8,128)(2,1)}, bf16[128,1024]{1,0:T(8,128)(2,1)}, bf16[128,1024]{1,0:T(8,128)(2,1)}, ...) | async-done | bytes 3932176 | tf_op jit(solution)/shard_map/psum | solution.py:276
  (254 shorter events, 249.5 us)
Async XLA Ops:
  7.2 27.8 %copy-start.15 = (bf16[512,1024]{1,0:T(8,128)(2,1)S(1)}, bf16[512,1024]{1,0:T(8,128)(2,1)}, u32[]{:S(2)}) copy-start(bf16[512,1024]{1,0:T(8,128)(2,1)} %param.13) | copy-start | bytes 3145732
  7.2 68.5 %all-gather.12.cloned.1.call-start = ((), (), s32[]{:S(2)}) async-start(), calls=%async_computation.8 | async-start | bytes 2359296 | tf_op jit(solution)/shard_map/all_gather | solution.py:116
  7.9 104.8 %all-gather.10.cloned.1.call-start = ((), (), s32[]{:S(2)}) async-start(), calls=%async_computation.7 | async-start | bytes 2359296 | tf_op jit(solution)/shard_map/all_gather | solution.py:117
  8.7 178.1 %all-gather.14.cloned.1.call-start = ((), (), s32[]{:S(2)}) async-start(), calls=%async_computation.9 | async-start | bytes 4718592 | tf_op jit(solution)/shard_map/all_gather | solution.py:115
  9.4 27.7 %copy-start.57 = (bf16[16]{0:T(256)(128)(2,1)S(1)}, bf16[16]{0:T(256)(128)(2,1)}, u32[]{:S(2)}) copy-start(bf16[16]{0:T(256)(128)(2,1)} %param.17) | copy-start | bytes 100
  9.4 27.9 %copy-start.58 = (bf16[16]{0:T(256)(128)(2,1)S(1)}, bf16[16]{0:T(256)(128)(2,1)}, u32[]{:S(2)}) copy-start(bf16[16]{0:T(256)(128)(2,1)} %param.16) | copy-start | bytes 100
  9.5 251.0 %all-gather.16.cloned.1.call-start = ((), (), s32[]{:S(2)}) async-start(), calls=%async_computation.10 | async-start | bytes 4718592 | tf_op jit(solution)/shard_map/all_gather | solution.py:118
  10.0 349.8 %all-gather.18.cloned.1.call-start = ((), (), s32[]{:S(2)}) async-start(), calls=%async_computation.11 | async-start | bytes 7077888 | tf_op jit(solution)/shard_map/all_gather | solution.py:156
  10.6 46.5 %copy-start.53 = (bf16[128]{0:T(256)(128)(2,1)S(1)}, bf16[128]{0:T(256)(128)(2,1)}, u32[]{:S(2)}) copy-start(bf16[128]{0:T(256)(128)(2,1)} %param.22) | copy-start | bytes 772
  10.6 448.4 %all-gather.20.cloned.1.call-start = ((), (), s32[]{:S(2)}) async-start(), calls=%async_computation.12 | async-start | bytes 7077888 | tf_op jit(solution)/shard_map/all_gather | solution.py:157
  11.2 547.3 %all-gather.22.cloned.1.call-start = ((), (), s32[]{:S(2)}) async-start(), calls=%async_computation.13 | async-start | bytes 7077888 | tf_op jit(solution)/shard_map/all_gather | solution.py:158
  12.0 736.0 %reduce-scatter.10.cloned.1.call-start = ((), (), s32[]{:S(2)}) async-start(), calls=%async_computation.15 | async-start | bytes 2359296 | tf_op jit(solution)/shard_map/reduce_scatter | solution.py:262
  35.0 151.8 %copy-start.41 = (f32[8,1,128]{2,1,0:T(1,128)}, f32[8,1,128]{2,1,0:T(1,128)S(1)}, u32[]{:S(2)}) copy-start(f32[8,1,128]{2,1,0:T(1,128)S(1)} %convert_element_type.224) | copy-start | bytes 12292
  35.9 150.9 %copy-start.46 = (f32[512]{0:T(512)}, f32[512]{0:T(512)S(1)}, u32[]{:S(2)}) copy-start(f32[512]{0:T(512)S(1)} %get-tuple-element.61) | copy-start | bytes 6148
  55.3 62.9 %copy-start.49 = (f32[128]{0:T(128)}, f32[128]{0:T(128)S(1)}, u32[]{:S(2)}) copy-start(f32[128]{0:T(128)S(1)} %convert_element_type.179) | copy-start | bytes 1540
  57.1 149.7 %copy-start.43 = (f32[128]{0:T(128)}, f32[128]{0:T(128)S(1)}, u32[]{:S(2)}) copy-start(f32[128]{0:T(128)S(1)} %convert_element_type.181) | copy-start | bytes 1540
  631.9 136.3 %reduce-scatter.12.cloned.1.call-start = ((), (), s32[]{:S(2)}) async-start(), calls=%async_computation.16 | async-start | bytes 2359296 | tf_op jit(solution)/shard_map/reduce_scatter | solution.py:265
  646.2 212.5 %reduce-scatter.8.cloned.1.call-start = ((), (), s32[]{:S(2)}) async-start(), calls=%async_computation.14 | async-start | bytes 4718592 | tf_op jit(solution)/shard_map/reduce_scatter | solution.py:259
  706.2 244.2 %reduce-scatter.14.cloned.1.call-start = ((), (), s32[]{:S(2)}) async-start(), calls=%async_computation.17 | async-start | bytes 4718592 | tf_op jit(solution)/shard_map/reduce_scatter | solution.py:268
  713.8 357.9 %reduce-scatter.16.cloned.1.call-start = ((), (), s32[]{:S(2)}) async-start(), calls=%async_computation.18 | async-start | bytes 7077888 | tf_op jit(solution)/shard_map/reduce_scatter | solution.py:192
  722.2 470.2 %reduce-scatter.18.cloned.1.call-start = ((), (), s32[]{:S(2)}) async-start(), calls=%async_computation.19 | async-start | bytes 7077888 | tf_op jit(solution)/shard_map/reduce_scatter | solution.py:195
  730.6 582.3 %reduce-scatter.20.cloned.1.call-start = ((), (), s32[]{:S(2)}) async-start(), calls=%async_computation.20 | async-start | bytes 7077888 | tf_op jit(solution)/shard_map/reduce_scatter | solution.py:198
  739.2 657.9 %all-reduce.12.cloned.1.call-start = ((), (), s32[]{:S(2)}) async-start(), calls=%async_computation.21 | async-start | bytes 7864320 | tf_op jit(solution)/shard_map/psum | solution.py:276
  1312.9 37.1 %copy-start.45 = (f32[512]{0:T(512)S(1)}, f32[512]{0:T(512)}, u32[]{:S(2)}) copy-start(f32[512]{0:T(512)} %get-tuple-element.60) | copy-start | bytes 6148
  (53 other events, 252.3 us)
Sparse Core Ops, SparseCore 0:
  10.2 52.4 all-gather.11
  64.7 47.9 all-gather.9
  114.8 71.8 all-gather.13
  188.7 71.6 all-gather.15
  262.5 97.2 all-gather.17
  361.8 97.2 all-gather.19
  461.2 97.2 all-gather.21
  632.0 65.8 reduce-scatter.9
  701.4 66.7 reduce-scatter.11
  771.7 86.9 reduce-scatter.7
  862.8 87.6 reduce-scatter.13
  953.9 117.7 reduce-scatter.15
  1075.2 117.0 reduce-scatter.17
  1195.8 117.0 reduce-scatter.19
  1315.6 81.5 all-reduce.11
where the time goes:
time: 1420 us; the launch traced here: 1410 us
  waiting for transfers between devices  996 us (70%)
  matrix products  177 us (12%)
  blocking collectives  84.4 us (6%)
  other arithmetic  75 us (5%)
  local copies, waits for them, and re-layouts  63.7 us (4%)
  between operations  16.9 us (1%)
    reduce_scatter x1, waiting for transfers between devices, shards(): lax.psum_scatter(gate_grad.astype(jnp.bfloat16), 'shard', scatter_dimensi...  121 us
    reduce_scatter x1, waiting for transfers between devices, shards(): lax.psum_scatter(up_grad.astype(jnp.bfloat16), 'shard', scatter_dimension...  121 us
    reduce_scatter x1, waiting for transfers between devices, shards(): lax.psum_scatter(down_grad.astype(jnp.bfloat16), 'shard', scatter_dimensi...  121 us
    reduce_scatter x1, waiting for transfers between devices, shards(): lax.psum_scatter(out_grad.astype(jnp.bfloat16), 'shard', scatter_dimensio...  91.8 us
    all_gather x1, waiting for transfers between devices, shards(): lax.all_gather(gate_proj, 'shard', axis=0, tiled=True)  91.2 us
    reduce_scatter x1, waiting for transfers between devices, shards(): lax.psum_scatter(query_grad.astype(jnp.bfloat16), 'shard', scatter_dimens...  90.5 us
    all_gather x1, waiting for transfers between devices, shards(): lax.all_gather(down_proj, 'shard', axis=0, tiled=True)  90.2 us
    all_gather x1, waiting for transfers between devices, shards(): lax.all_gather(up_proj, 'shard', axis=0, tiled=True)  90.1 us
  transfers between devices with their start and end apart: 15, of which 13 were waited for; matrix products, arithmetic and copies ran while one was open for 16% of the time, Pallas kernels for 0%

commit v1 on v0

v1 whole, which is shorter than its diff:
```python
import jax
import jax.numpy as jnp
from jax import lax
from jax.sharding import PartitionSpec as P

EPS = 1e-06
THETA = 1000000.0


def product(left, right):
    return jnp.dot(left, right, preferred_element_type=jnp.float32)


def left_product(left, right):
    return lax.dot_general(
        left, right, (((0,), (0,)), ((), ())), preferred_element_type=jnp.float32
    )


def right_product(left, right):
    return lax.dot_general(
        left, right, (((1,), (1,)), ((), ())), preferred_element_type=jnp.float32
    )


def rotary_tables(length, width):
    half_width = width // 2
    frequency = THETA ** (-(jnp.arange(half_width, dtype=jnp.float32) * 2.0) / width)
    angles = jnp.arange(length, dtype=jnp.float32)[:, None] * frequency[None, :]
    angles = jnp.concatenate([angles, angles], axis=1)
    return (jnp.cos(angles)[:, None, :], jnp.sin(angles)[:, None, :])


def rotate(values):
    half_width = values.shape[-1] // 2
    return jnp.concatenate([-values[..., half_width:], values[..., :half_width]], axis=-1)


def rotate_back(values):
    half_width = values.shape[-1] // 2
    return jnp.concatenate([values[..., half_width:], -values[..., :half_width]], axis=-1)


def inverse_rms(values):
    return lax.rsqrt(jnp.mean(values * values, axis=-1, keepdims=True) + EPS)


def norm_back(grads, values, inverse, gain):
    weighted = grads * gain
    return inverse * weighted - values * (inverse * inverse * inverse) * jnp.mean(
        weighted * values, axis=-1, keepdims=True
    )


def masked_scores(query_b, key_b):
    head_size = query_b.shape[-1]
    length = query_b.shape[0]
    scores = jnp.einsum(
        "qgjd,kgd->gjqk", query_b, key_b, preferred_element_type=jnp.float32
    ) * head_size ** (-0.5)
    causal = jnp.arange(length)[:, None] >= jnp.arange(length)[None, :]
    return jnp.where(causal, scores, -1e30)


def attend(query_b, key_b, value_b):
    scores = masked_scores(query_b, key_b)
    highest = jnp.max(scores, axis=-1, keepdims=True)
    powers = jnp.exp(scores - highest)
    totals = jnp.sum(powers, axis=-1, keepdims=True)
    probs_b = (powers / totals).astype(jnp.bfloat16)
    mixed = jnp.einsum("gjqk,kgd->qgjd", probs_b, value_b, preferred_element_type=jnp.float32)
    return (mixed, highest + jnp.log(totals))


def attend_back(query_b, key_b, value_b, log_totals, grad_mixed):
    head_size = query_b.shape[-1]
    probs = jnp.exp(masked_scores(query_b, key_b) - log_totals)
    probs_b = probs.astype(jnp.bfloat16)
    grad_probs = jnp.einsum(
        "qgjd,kgd->gjqk", grad_mixed, value_b, preferred_element_type=jnp.float32
    )
    value_grad = jnp.einsum(
        "gjqk,qgjd->kgd", probs_b, grad_mixed, preferred_element_type=jnp.float32
    )
    grad_scores = probs * (grad_probs - jnp.sum(probs * grad_probs, axis=-1, keepdims=True))
    grad_scores = grad_scores.astype(jnp.bfloat16)
    grad_qrot = jnp.einsum(
        "gjqk,kgd->qgjd", grad_scores, key_b, preferred_element_type=jnp.float32
    ) * head_size ** (-0.5)
    grad_krot = jnp.einsum(
        "gjqk,qgjd->kgd", grad_scores, query_b, preferred_element_type=jnp.float32
    ) * head_size ** (-0.5)
    return (grad_qrot, grad_krot, value_grad)


def sibling_pairs(count):
    return [(i, i ^ 1) for i in range(count)]


def from_sibling(values):
    return lax.ppermute(values, "rep", sibling_pairs(lax.axis_size("rep")))


def half_columns(values, core):
    width = values.shape[1] // 2
    return lax.dynamic_slice_in_dim(values, core * width, width, axis=1)


def in_order(mine, other, core):
    first = core == 0
    return jnp.concatenate([jnp.where(first, mine, other), jnp.where(first, other, mine)], axis=-1)


def gather_pair(block):
    mine = lax.all_gather(block, "shard", axis=0, tiled=True)
    return (mine, from_sibling(mine))


def scatter_pair(mine, other):
    received = from_sibling(other.astype(jnp.bfloat16))
    pair = (mine + received.astype(jnp.float32)).astype(jnp.bfloat16)
    part = lax.psum_scatter(pair, "shard", scatter_dimension=0, tiled=True)
    count = lax.axis_size("rep")
    groups = [list(range(c, count, 2)) for c in range(2)]
    return lax.psum(part, "rep", axis_index_groups=groups)


def shards(
    tokens,
    cotangent,
    attn_gain,
    query_gain,
    key_gain,
    query_proj,
    key_proj,
    value_proj,
    out_proj,
    mlp_gain,
    gate_proj,
    up_proj,
    down_proj,
):
    core = lax.rem(lax.axis_index("rep"), 2)
    size = lax.axis_size("shard")
    width = tokens.shape[1]
    head_size = query_gain.shape[0] * size
    query_heads = query_proj.shape[1] // head_size
    key_heads = key_proj.shape[1] // head_size
    group_size = query_heads // key_heads
    length = tokens.shape[0]
    gains = lax.all_gather(
        jnp.concatenate([attn_gain, mlp_gain, query_gain, key_gain]), "shard", axis=0, tiled=False
    ).astype(jnp.float32)
    step = width // size
    small = head_size // size
    attn_scale = gains[:, :step].reshape(width)
    mlp_scale = gains[:, step : 2 * step].reshape(width)
    query_scale = gains[:, 2 * step : 2 * step + small].reshape(head_size)
    key_scale = gains[:, 2 * step + small :].reshape(head_size)
    qkv = gather_pair(
        jnp.concatenate([half_columns(w, core) for w in (query_proj, key_proj, value_proj)], axis=1)
    )
    outs = gather_pair(half_columns(out_proj, core))
    gate_up = gather_pair(
        jnp.concatenate([half_columns(w, core) for w in (gate_proj, up_proj)], axis=1)
    )
    downs = gather_pair(half_columns(down_proj, core))

    q_half = query_proj.shape[1] // 2
    k_half = key_proj.shape[1] // 2
    ff_half = gate_proj.shape[1] // 2
    inputs = tokens.astype(jnp.float32)
    cosine, sine = rotary_tables(length, head_size)
    inv_one = inverse_rms(inputs)
    normed = (inputs * inv_one * attn_scale).astype(jnp.bfloat16)
    raws = [product(normed, w) for w in qkv]
    query_raw = jnp.concatenate([r[:, :q_half] for r in raws], axis=1).reshape(
        length, query_heads, head_size
    )
    key_raw = jnp.concatenate([r[:, q_half : q_half + k_half] for r in raws], axis=1).reshape(
        length, key_heads, head_size
    )
    value_b = (
        jnp.concatenate([r[:, q_half + k_half :] for r in raws], axis=1)
        .astype(jnp.bfloat16)
        .reshape(length, key_heads, head_size)
    )
    inv_query = inverse_rms(query_raw)
    inv_key = inverse_rms(key_raw)
    query_normed = query_raw * inv_query * query_scale
    key_normed = key_raw * inv_key * key_scale
    query_rot = (
        (query_normed * cosine + rotate(query_normed) * sine)
        .astype(jnp.bfloat16)
        .reshape(length, key_heads, group_size, head_size)
    )
    key_rot = (key_normed * cosine + rotate(key_normed) * sine).astype(jnp.bfloat16)
    mixed, log_totals = attend(query_rot, key_rot, value_b)
    mixed_b = mixed.reshape(length, query_heads * head_size).astype(jnp.bfloat16)
    mixed_b = in_order(mixed_b[:, :q_half], mixed_b[:, q_half:], core)
    middle = inputs + in_order(product(mixed_b, outs[0]), product(mixed_b, outs[1]), core)
    inv_two = inverse_rms(middle)
    inner = (middle * inv_two * mlp_scale).astype(jnp.bfloat16)
    cot = [half_columns(cotangent, core), half_columns(cotangent, 1 - core)]
    gates_ups = [product(inner, w) for w in gate_up]
    gate_values = [v[:, :ff_half] for v in gates_ups]
    up_values = [v[:, ff_half:] for v in gates_ups]
    hiddens = [
        (jax.nn.silu(g) * u).astype(jnp.bfloat16) for g, u in zip(gate_values, up_values)
    ]
    hidden = in_order(hiddens[0], hiddens[1], core)
    layer_out = (
        middle + in_order(product(hidden, downs[0]), product(hidden, downs[1]), core)
    ).astype(jnp.bfloat16)
    grad_hidden = right_product(cot[0], downs[0]) + right_product(cot[1], downs[1])
    grad_hiddens = [half_columns(grad_hidden, core), half_columns(grad_hidden, 1 - core)]
    down_part = scatter_pair(left_product(hidden, cot[0]), left_product(hidden, cot[1]))
    grads = []
    for g, u, grad in zip(gate_values, up_values, grad_hiddens):
        sigmoid = jax.nn.sigmoid(g)
        grads.append(
            jnp.concatenate(
                [
                    (grad * u * (sigmoid + g * sigmoid * (1.0 - sigmoid))).astype(jnp.bfloat16),
                    (grad * (g * sigmoid)).astype(jnp.bfloat16),
                ],
                axis=1,
            )
        )
    gate_up_part = scatter_pair(left_product(inner, grads[0]), left_product(inner, grads[1]))
    grad_inner = right_product(grads[0], gate_up[0]) + right_product(grads[1], gate_up[1])
    mlp_gain_grad = jnp.sum(grad_inner * middle * inv_two, axis=0)
    grad_middle = cotangent.astype(jnp.float32) + norm_back(grad_inner, middle, inv_two, mlp_scale)
    grad_attn = grad_middle.astype(jnp.bfloat16)
    grad_attns = [half_columns(grad_attn, core), half_columns(grad_attn, 1 - core)]
    out_part = scatter_pair(
        left_product(mixed_b, grad_attns[0]), left_product(mixed_b, grad_attns[1])
    )
    grad_mixed = (
        right_product(grad_attns[0], outs[0]) + right_product(grad_attns[1], outs[1])
    ).astype(jnp.bfloat16)
    grad_mixed = jnp.concatenate(
        [half_columns(grad_mixed, core), half_columns(grad_mixed, 1 - core)], axis=1
    ).reshape(length, key_heads, group_size, head_size)
    grad_qrot, grad_krot, value_grad = attend_back(
        query_rot, key_rot, value_b, log_totals, grad_mixed
    )
    grad_qrot = grad_qrot.reshape(length, query_heads, head_size)
    grad_qnorm = grad_qrot * cosine + rotate_back(grad_qrot * sine)
    grad_knorm = grad_krot * cosine + rotate_back(grad_krot * sine)
    query_gain_grad = jnp.sum(grad_qnorm * query_raw * inv_query, axis=(0, 1))
    key_gain_grad = jnp.sum(grad_knorm * key_raw * inv_key, axis=(0, 1))
    grad_query = norm_back(grad_qnorm, query_raw, inv_query, query_scale)
    grad_query = grad_query.astype(jnp.bfloat16).reshape(length, query_heads * head_size)
    grad_key = norm_back(grad_knorm, key_raw, inv_key, key_scale)
    grad_key = grad_key.astype(jnp.bfloat16).reshape(length, key_heads * head_size)
    value_grad = value_grad.astype(jnp.bfloat16).reshape(length, key_heads * head_size)
    grad_qkv = [
        jnp.concatenate([grad_query[:, :q_half], grad_key[:, :k_half], value_grad[:, :k_half]], 1),
        jnp.concatenate([grad_query[:, q_half:], grad_key[:, k_half:], value_grad[:, k_half:]], 1),
    ]
    qkv_part = scatter_pair(left_product(normed, grad_qkv[0]), left_product(normed, grad_qkv[1]))
    grad_normed = right_product(grad_qkv[0], qkv[0]) + right_product(grad_qkv[1], qkv[1])
    attn_gain_grad = jnp.sum(grad_normed * inputs * inv_one, axis=0)
    tokens_grad = grad_middle + norm_back(grad_normed, inputs, inv_one, attn_scale)

    gain_grads = jnp.concatenate(
        [
            attn_gain_grad.reshape(size, step),
            mlp_gain_grad.reshape(size, step),
            query_gain_grad.reshape(size, small),
            key_gain_grad.reshape(size, small),
        ],
        axis=1,
    )
    gain_sums = lax.psum(gain_grads, ("rep", "shard"))
    gain_sums = lax.dynamic_index_in_dim(
        gain_sums, lax.axis_index("shard"), axis=0, keepdims=False
    )

    parts = [qkv_part, out_part, gate_up_part, down_part]
    others = [from_sibling(p) for p in parts]

    def whole(index, start, stop):
        return in_order(
            parts[index][:, start:stop].astype(jnp.float32),
            others[index][:, start:stop].astype(jnp.float32),
            core,
        )

    return (
        layer_out,
        tokens_grad,
        gain_sums[:step],
        gain_sums[2 * step : 2 * step + small],
        gain_sums[2 * step + small :],
        whole(0, 0, q_half),
        whole(0, q_half, q_half + k_half),
        whole(0, q_half + k_half, q_half + 2 * k_half),
        whole(1, 0, width // 2),
        gain_sums[step : 2 * step],
        whole(2, 0, ff_half),
        whole(2, ff_half, 2 * ff_half),
        whole(3, 0, width // 2),
    )


def solution(mesh):
    in_specs = (
        P(("rep", "shard"), None),
        P(("rep", "shard"), None),
        P("shard"),
        P("shard"),
        P("shard"),
        P("shard", None),
        P("shard", None),
        P("shard", None),
        P("shard", None),
        P("shard"),
        P("shard", None),
        P("shard", None),
        P("shard", None),
    )
    out_specs = (
        P(("rep", "shard"), None),
        P(("rep", "shard"), None),
        P("shard"),
        P("shard"),
        P("shard"),
        P("shard", None),
        P("shard", None),
        P("shard", None),
        P("shard", None),
        P("shard"),
        P("shard", None),
        P("shard", None),
        P("shard", None),
    )
    return jax.shard_map(shards, mesh=mesh, in_specs=in_specs, out_specs=out_specs, check_vma=False)
```

time: 1420 us -> 966 us (0.68)
  waiting for transfers between devices: 996 us -> 521 us
  local copies, waits for them, and re-layouts: 63.7 us -> 109 us
  blocking collectives: 84.4 us -> 59 us
  matrix products: 177 us -> 159 us
    reduce_scatter x7 -> x4, waiting for transfers between devices: 565 us -> 235 us  [scatter_pair(): part = lax.psum_scatter(pair, 'shard', scatter_dimension=0, tiled=True)]
    all_gather x7 -> x4, waiting for transfers between devices: 390 us -> 226 us  [gather_pair(): mine = lax.all_gather(block, 'shard', axis=0, tiled=True)]
    all_gather x2 -> x0, blocking collectives: 40.2 us -> none  [the longest x1 22.2 us: shards(): lax.all_gather(attn_gain, 'shard', axis=0, tiled=True)]
    psum x1, blocking collectives: 6.75 us -> 39.5 us  [shards(): gain_sums = lax.psum(gain_grads, ('rep', 'shard'))]
    unnamed x135 -> x252, local copies, waits for them, and re-layouts: 21.5 us -> 49.5 us
    unnamed x2 -> x1, blocking collectives: 37.5 us -> 19.5 us
    ppermute x0 -> x12, waiting for transfers between devices: none -> 15.7 us  [from_sibling(): return lax.ppermute(values, 'rep', sibling_pairs(lax.axis_size('rep')))]
    dot_general x7 -> x8, matrix products: 44 us -> 29.3 us  [product(): return jnp.dot(left, right, preferred_element_type=jnp.float32)]
  transfers between devices with their start and end apart: 15 -> 21, of which waited for: 13 -> 10; matrix products, arithmetic and copies ran while one was open for 16% -> 33% of each run, Pallas kernels for 0% -> 0%
where the time goes in v1:
time: 966 us; the launch traced here: 955 us
  waiting for transfers between devices  521 us (54%)
  matrix products  159 us (16%)
  local copies, waits for them, and re-layouts  109 us (11%)
  other arithmetic  88.2 us (9%)
  blocking collectives  59 us (6%)
  between operations  16.5 us (2%)
    reduce_scatter x4, waiting for transfers between devices, scatter_pair(): part = lax.psum_scatter(pair, 'shard', scatter_dimension=0, tiled=True)  235 us
    all_gather x4, waiting for transfers between devices, gather_pair(): mine = lax.all_gather(block, 'shard', axis=0, tiled=True)  226 us
    unnamed x252, local copies, waits for them, and re-layouts  49.5 us
    psum x1, waiting for transfers between devices, scatter_pair(): return lax.psum(part, 'rep', axis_index_groups=groups)  44.1 us
    dot_general x8, matrix products, right_product(): lax.dot_general(left, right, (((1,), (1,)), ((), ())), preferred_element_...  41.1 us
    psum x1, blocking collectives, shards(): gain_sums = lax.psum(gain_grads, ('rep', 'shard'))  39.5 us
    dot_general x8, matrix products, left_product(): lax.dot_general(left, right, (((0,), (0,)), ((), ())), preferred_element_...  39.5 us
    dot_general x8, matrix products, product(): return jnp.dot(left, right, preferred_element_type=jnp.float32)  29.3 us
  transfers between devices with their start and end apart: 21, of which 10 were waited for; matrix products, arithmetic and copies ran while one was open for 33% of the time, Pallas kernels for 0%

profile of v1, /device:TPU:0, one launch (start us, length us, event | category | flops | bytes accessed | tf_op | source)
XLA Modules:
  0.0 955.2 jit_solution(10393868990881930161)
XLA Ops:
  14.2 72.6 %all-gather.6.cloned.1.call-done = bf16[1024,2048]{1,0:T(8,128)(2,1)} async-done(((bf16[128,2048]{1,0:T(8,128)(2,1)}), bf16[1024,2048]{1,0:T(8,128)(2,1)}) %all-gather.6.cloned.1.call-update) | async-done | bytes 4194320 | tf_op jit(solution)/shard_map/all_gather | solution.py:115
  89.7 58.6 %all-gather.12.cloned.1.call-done = bf16[3072,512]{1,0:T(8,128)(2,1)} async-done(((bf16[384,512]{1,0:T(8,128)(2,1)}), bf16[3072,512]{1,0:T(8,128)(2,1)}) %all-gather.12.cloned.1.call-update) | async-done | bytes 3145744 | tf_op jit(solution)/shard_map/all_gather | solution.py:115
  148.7 19.5 %all-reduce = bf16[2304]{0:T(1024)(128)(2,1)S(1)} all-reduce(bf16[2304]{0:T(1024)(128)(2,1)S(1)} %dynamic-update-slice), channel_id=2, replica_groups=mesh['rep'=4,'shard'=8] {'shard'}, use_global_device_ids=true, to_apply=%add | all-reduce | flops 2304 | bytes 9216
  181.1 18.1 %all-gather.8.cloned.1.call-done = bf16[2048,512]{1,0:T(8,128)(2,1)} async-done(((bf16[256,512]{1,0:T(8,128)(2,1)}), bf16[2048,512]{1,0:T(8,128)(2,1)}) %all-gather.8.cloned.1.call-update) | async-done | bytes 2097168 | tf_op jit(solution)/shard_map/all_gather | solution.py:115
  199.3 6.5 fusion.55
  216.8 6.5 convolution_add_fusion
  223.3 76.1 %all-gather.10.cloned.1.call-done = bf16[1024,3072]{1,0:T(8,128)(2,1)} async-done(((bf16[128,3072]{1,0:T(8,128)(2,1)}), bf16[1024,3072]{1,0:T(8,128)(2,1)}) %all-gather.10.cloned.1.call-update) | async-done | bytes 6291472 | tf_op jit(solution)/shard_map/all_gather | solution.py:115
  343.0 7.5 fusion.97
  359.6 8.2 fusion.3
  367.8 8.3 fusion.35
  411.4 7.3 multiply_reduce_fusion.2
  430.9 14.6 %fusion = (f32[8,2,512]{2,1,0:T(2,128)S(1)}, f32[8,512,512,2]{2,1,3,0:T(8,128)}) fusion(f32[8,2,512,512]{2,3,1,0:T(8,128)} %get-tuple-element.152, f32[8,2,512]{2,1,0:T(2,128)S(1)} %bitcast.183, bf16[512,8,2,128]{0,3,2,1:T(8,128)(2,1)} %bitcast.158, bf16[512,4,128]{0,2,1:T(8,128)(2,1)} %bitcast.181, bf16[512,4,128]{0,2,1:T(8,128)(2,1)} %bitcast.179), kind=kOutput, calls=%fused_computation.2 | convolution fusion | flops 1088413696 | bytes 36765696 | tf_op jit(solution)/shard_map/qgjd,kgd->gjqk/dot_general | solution.py:79
  448.3 8.4 fusion.2
  497.7 8.8 bitcast_convert_fusion
  507.8 6.3 add_convert_fusion.2
  518.8 8.3 fusion.10
  541.4 6.7 add_convert_fusion.1
  555.7 9.8 %collective-permute-done.8 = bf16[1024,3072]{1,0:T(8,128)(2,1)S(1)} collective-permute-done((bf16[1024,3072]{1,0:T(8,128)(2,1)S(1)}, bf16[1024,3072]{1,0:T(8,128)(2,1)S(1)}, u32[]{:S(2)}, u32[]{:S(2)}) %collective-permute-start.8) | collective-permute-done | bytes 6291488 | tf_op jit(solution)/shard_map/ppermute | solution.py:101
  594.5 23.0 %reduce-scatter.11.cloned.1.call-done = bf16[384,512]{1,0:T(8,128)(2,1)} async-done(((bf16[3072,512]{1,0:T(8,128)(2,1)}), bf16[384,512]{1,0:T(8,128)(2,1)}) %reduce-scatter.11.cloned.1.call-update) | async-done | bytes 393232 | tf_op jit(solution)/shard_map/reduce_scatter | solution.py:122
  617.4 90.7 %reduce-scatter.5.cloned.1.call-done = bf16[128,2048]{1,0:T(8,128)(2,1)} async-done(((bf16[1024,2048]{1,0:T(8,128)(2,1)}), bf16[128,2048]{1,0:T(8,128)(2,1)}) %reduce-scatter.5.cloned.1.call-update) | async-done | bytes 524304 | tf_op jit(solution)/shard_map/reduce_scatter | solution.py:122
  708.1 121.7 %reduce-scatter.9.cloned.1.call-done = bf16[128,3072]{1,0:T(8,128)(2,1)} async-done(((bf16[1024,3072]{1,0:T(8,128)(2,1)}), bf16[128,3072]{1,0:T(8,128)(2,1)}) %reduce-scatter.9.cloned.1.call-update) | async-done | bytes 786448 | tf_op jit(solution)/shard_map/reduce_scatter | solution.py:122
  829.8 6.5 fusion.15
  848.1 44.1 %all-reduce.4.cloned.1.call-done = (bf16[128,2048]{1,0:T(8,128)(2,1)}, bf16[256,512]{1,0:T(8,128)(2,1)}, bf16[128,3072]{1,0:T(8,128)(2,1)}, bf16[384,512]{1,0:T(8,128)(2,1)}) async-done(((bf16[128,2048]{1,0:T(8,128)(2,1)}, bf16[256,512]{1,0:T(8,128)(2,1)}, bf16[128,3072]{1,0:T(8,128)(2,1)}, bf16[384,512]{1,0:T(8,128)(2,1)}), (bf16[128,2048]{1,0:T(8,128)(2,1)}, bf16[256,512]{1,0:T(8,128)(2,1)}, ...) | async-done | bytes 1966096 | tf_op jit(solution)/shard_map/psum | solution.py:125
  896.6 39.5 %psum.35 = f32[8,288]{1,0:T(8,128)S(1)} all-reduce(f32[8,288]{1,0:T(8,128)S(1)} %pad_maximum_fusion.34), channel_id=1, replica_groups=mesh['rep'=4,'shard'=8] {'rep','shard'}, use_global_device_ids=true, to_apply=%region_15.16 | all-reduce | flops 2304 | bytes 18432 | tf_op jit(solution)/shard_map/psum | solution.py:276
  (417 shorter events, 261.0 us)
Async XLA Ops:
  7.2 79.7 %all-gather.6.cloned.1.call-start = ((), (), s32[]{:S(2)}) async-start(), calls=%async_computation.4 | async-start | bytes 4718592 | tf_op jit(solution)/shard_map/all_gather | solution.py:115
  10.2 138.1 %all-gather.12.cloned.1.call-start = ((), (), s32[]{:S(2)}) async-start(), calls=%async_computation.7 | async-start | bytes 3538944 | tf_op jit(solution)/shard_map/all_gather | solution.py:115
  11.1 188.2 %all-gather.8.cloned.1.call-start = ((), (), s32[]{:S(2)}) async-start(), calls=%async_computation.5 | async-start | bytes 2359296 | tf_op jit(solution)/shard_map/all_gather | solution.py:115
  12.0 287.5 %all-gather.10.cloned.1.call-start = ((), (), s32[]{:S(2)}) async-start(), calls=%async_computation.6 | async-start | bytes 7077888 | tf_op jit(solution)/shard_map/all_gather | solution.py:115
  14.2 580.3 %reduce-scatter.7.cloned.1.call-start = ((), (), s32[]{:S(2)}) async-start(), calls=%async_computation.9 | async-start | bytes 2359296 | tf_op jit(solution)/shard_map/reduce_scatter | solution.py:122
  86.9 212.5 %collective-permute-start = (bf16[1024,2048]{1,0:T(8,128)(2,1)}, bf16[1024,2048]{1,0:T(8,128)(2,1)}, u32[]{:S(2)}, u32[]{:S(2)}) collective-permute-start(bf16[1024,2048]{1,0:T(8,128)(2,1)} %all-gather.6.cloned.1.call-done), channel_id=1, source_target_pairs={{0,8},{8,0},{16,24},{24,16},{1,9},{9,1},{17,25},{25,17},{2,10},{10... | collective-permute-start | bytes 12582920 | tf_op jit(solution)/shard_map/ppermute | solution.py:101
  88.4 211.0 %copy-start.9 = (bf16[512,1024]{0,1:T(8,128)(2,1)}, bf16[512,1024]{0,1:T(8,128)(2,1)S(1)}, u32[]{:S(2)}) copy-start(bf16[512,1024]{0,1:T(8,128)(2,1)S(1)} %copy.143) | copy-start | bytes 3145732
  148.4 68.5 %collective-permute-start.3 = (bf16[3072,512]{1,0:T(8,128)(2,1)}, bf16[3072,512]{1,0:T(8,128)(2,1)}, u32[]{:S(2)}, u32[]{:S(2)}) collective-permute-start(bf16[3072,512]{1,0:T(8,128)(2,1)} %all-gather.12.cloned.1.call-done), channel_id=1, source_target_pairs={{0,8},{8,0},{16,24},{24,16},{1,9},{9,1},{17,25},{25,17},{2,10},{10... | collective-permute-start | bytes 9437192 | tf_op jit(solution)/shard_map/ppermute | solution.py:101
  181.1 237.6 %copy-start.89 = (f32[1024]{0:T(1024)}, f32[1024]{0:T(1024)S(1)}, u32[]{:S(2)}) copy-start(f32[1024]{0:T(1024)S(1)} %get-tuple-element.143) | copy-start | bytes 12292
  199.3 180.5 %collective-permute-start.1 = (bf16[2048,512]{1,0:T(8,128)(2,1)}, bf16[2048,512]{1,0:T(8,128)(2,1)}, u32[]{:S(2)}, u32[]{:S(2)}) collective-permute-start(bf16[2048,512]{1,0:T(8,128)(2,1)} %all-gather.8.cloned.1.call-done), channel_id=1, source_target_pairs={{0,8},{8,0},{16,24},{24,16},{1,9},{9,1},{17,25},{25,17},{2,10},{10... | collective-permute-start | bytes 6291464 | tf_op jit(solution)/shard_map/ppermute | solution.py:101
  299.4 87.8 %collective-permute-start.2 = (bf16[1024,3072]{1,0:T(8,128)(2,1)}, bf16[1024,3072]{1,0:T(8,128)(2,1)}, u32[]{:S(2)}, u32[]{:S(2)}) collective-permute-start(bf16[1024,3072]{1,0:T(8,128)(2,1)} %all-gather.10.cloned.1.call-done), channel_id=1, source_target_pairs={{0,8},{8,0},{16,24},{24,16},{1,9},{9,1},{17,25},{25,17},{2,10},{10... | collective-permute-start | bytes 18874376 | tf_op jit(solution)/shard_map/ppermute | solution.py:101
  400.7 107.0 %collective-permute-start.10 = (bf16[3072,512]{1,0:T(8,128)(2,1)}, bf16[3072,512]{1,0:T(8,128)(2,1)}, u32[]{:S(2)}, u32[]{:S(2)}) collective-permute-start(bf16[3072,512]{1,0:T(8,128)(2,1)} %convolution_convert_fusion.1), channel_id=1, source_target_pairs={{0,8},{8,0},{16,24},{24,16},{1,9},{9,1},{17,25},{25,17},{2,10},{10... | collective-permute-start | bytes 9437192 | tf_op jit(solution)/shard_map/ppermute | solution.py:101
  423.7 46.4 %collective-permute-start.6 = (bf16[2048,512]{1,0:T(8,128)(2,1)}, bf16[2048,512]{1,0:T(8,128)(2,1)}, u32[]{:S(2)}, u32[]{:S(2)}) collective-permute-start(bf16[2048,512]{1,0:T(8,128)(2,1)} %convolution_convert_fusion.3), channel_id=1, source_target_pairs={{0,8},{8,0},{16,24},{24,16},{1,9},{9,1},{17,25},{25,17},{2,10},{10... | collective-permute-start | bytes 6291464 | tf_op jit(solution)/shard_map/ppermute | solution.py:101
  474.4 143.0 %reduce-scatter.11.cloned.1.call-start = ((), (), s32[]{:S(2)}) async-start(), calls=%async_computation.11 | async-start | bytes 3538944 | tf_op jit(solution)/shard_map/reduce_scatter | solution.py:122
  514.2 194.0 %reduce-scatter.5.cloned.1.call-start = ((), (), s32[]{:S(2)}) async-start(), calls=%async_computation.8 | async-start | bytes 4718592 | tf_op jit(solution)/shard_map/reduce_scatter | solution.py:122
  533.7 7.8 collective-permute-start.4
  548.2 281.6 %reduce-scatter.9.cloned.1.call-start = ((), (), s32[]{:S(2)}) async-start(), calls=%async_computation.10 | async-start | bytes 7077888 | tf_op jit(solution)/shard_map/reduce_scatter | solution.py:122
  555.3 10.2 %collective-permute-start.8 = (bf16[1024,3072]{1,0:T(8,128)(2,1)S(1)}, bf16[1024,3072]{1,0:T(8,128)(2,1)S(1)}, u32[]{:S(2)}, u32[]{:S(2)}) collective-permute-start(bf16[1024,3072]{1,0:T(8,128)(2,1)S(1)} %convolution_convert_fusion), channel_id=1, source_target_pairs={{0,8},{8,0},{16,24},{24,16},{1,9},{9,1},{17,25},{25,17},{2,10},{10... | collective-permute-start | bytes 18874376 | tf_op jit(solution)/shard_map/ppermute | solution.py:101
  571.2 320.9 %all-reduce.4.cloned.1.call-start = ((), (), s32[]{:S(2)}) async-start(), calls=%async_computation.12 | async-start | bytes 3932160 | tf_op jit(solution)/shard_map/psum | solution.py:125
  588.2 241.6 %copy-start.83 = (f32[512,8,2]{0,2,1:T(2,128)S(1)}, f32[512,8,2]{0,2,1:T(2,128)}, u32[]{:S(2)}) copy-start(f32[512,8,2]{0,2,1:T(2,128)} %copy-done.82) | copy-start | bytes 98308
  892.2 45.7 %collective-permute-start.7 = (bf16[256,512]{1,0:T(8,128)(2,1)}, bf16[256,512]{1,0:T(8,128)(2,1)}, u32[]{:S(2)}, u32[]{:S(2)}) collective-permute-start(bf16[256,512]{1,0:T(8,128)(2,1)} %get-tuple-element.72), channel_id=1, source_target_pairs={{0,8},{8,0},{16,24},{24,16},{1,9},{9,1},{17,25},{25,17},{2,10},{10... | collective-permute-start | bytes 786440 | tf_op jit(solution)/shard_map/ppermute | solution.py:101
  937.3 2.8 collective-permute-start.11
  937.3 8.1 collective-permute-start.9
  937.8 4.6 collective-permute-start.5
  (117 other events, 2123.5 us)
Sparse Core Ops, SparseCore 0:
  10.7 76.0 all-gather.5
  89.6 58.7 all-gather.11
  151.1 48.1 all-gather.7
  201.9 97.5 all-gather.9
  474.6 66.0 reduce-scatter.6
  544.1 73.2 reduce-scatter.10
  621.1 87.0 reduce-scatter.4
  712.1 117.6 reduce-scatter.8
  832.4 59.7 all-reduce.3

commit v2 on v1

--- a/solution.py
+++ b/solution.py
@@ -1,6 +1,10 @@
+import functools
+
 import jax
 import jax.numpy as jnp
 from jax import lax
+from jax.experimental import pallas as pl
+from jax.experimental.pallas import tpu as pltpu
 from jax.sharding import PartitionSpec as P
 
 EPS = 1e-06
@@ -123,6 +127,237 @@
     count = lax.axis_size("rep")
     groups = [list(range(c, count, 2)) for c in range(2)]
     return lax.psum(part, "rep", axis_index_groups=groups)
+
+
+MESH = pl.DeviceIdType.MESH
+
+
+def ring_member(place, size):
+    place = lax.rem(place + 2 * size, size)
+    back = place // (size // 2)
+    return (1 - back) * (2 * place) + back * (2 * (size - 1 - place) + 1)
+
+
+def ring_place(size):
+    index = lax.axis_index("shard")
+    odd = lax.rem(index, 2)
+    row = index // 2
+    return (1 - odd) * row + odd * (size - 1 - row)
+
+
+def sibling():
+    rep = lax.axis_index("rep")
+    return {"rep": rep + 1 - 2 * lax.rem(rep, 2)}
+
+
+def greet(devices):
+    barrier = pltpu.get_barrier_semaphore()
+    for device in devices:
+        pl.semaphore_signal(barrier, inc=1, device_id=device, device_id_type=MESH)
+    pl.semaphore_wait(barrier, len(devices))
+
+
+def rows_of(ref, index, way):
+    rows = ref.shape[1] // 2
+    return ref.at[index, pl.ds(way * rows, rows)]
+
+
+def gather_kernel(size, count, *refs):
+    blocks, mine, other = refs[:count], refs[count : 2 * count], refs[2 * count : 3 * count]
+    ring_send, ring_recv, pair_send, pair_recv, local = refs[3 * count :]
+    me = lax.axis_index("shard")
+    place = ring_place(size)
+    pair = sibling()
+    near = [{"shard": ring_member(place + 1, size)}, {"shard": ring_member(place - 1, size)}]
+    greet(near + [pair])
+
+    def send(src, dst, sems, step, way, i, device):
+        copy = pltpu.make_async_remote_copy(
+            src_ref=src,
+            dst_ref=dst,
+            send_sem=sems[0].at[step, way, i],
+            recv_sem=sems[1].at[step, way, i],
+            device_id=device,
+            device_id_type=MESH,
+        )
+        copy.start()
+        return copy
+
+    ring_sems, pair_sems = (ring_send, ring_recv), (pair_send, pair_recv)
+    ring, pairs, locals_ = {}, [], []
+    for step in range(size):
+        for i in range(count):
+            for way in range(2):
+                index = ring_member(place - step if way == 0 else place + step, size)
+                rows = blocks[i].shape[0] // 2
+                if step == 0:
+                    src = blocks[i].at[pl.ds(way * rows, rows)]
+                else:
+                    ring[step - 1, way, i].wait_recv()
+                    src = rows_of(mine[i], index, way)
+                if step < size - 1:
+                    ring[step, way, i] = send(
+                        src, rows_of(mine[i], index, way), ring_sems, step, way, i, near[way]
+                    )
+                pairs.append(
+                    send(src, rows_of(other[i], index, way), pair_sems, step, way, i, pair)
+                )
+        if step == 0:
+            for i in range(count):
+                copy = pltpu.make_async_copy(blocks[i], mine[i].at[me], local.at[i])
+                copy.start()
+                locals_.append(copy)
+    for copy in locals_:
+        copy.wait()
+    for copy in ring.values():
+        copy.wait_send()
+    for copy in pairs:
+        copy.wait()
+
+
+def ring_gather(blocks, size):
+    count = len(blocks)
+    shapes = [jax.ShapeDtypeStruct((size,) + b.shape, b.dtype) for b in blocks]
+    sems = pltpu.SemaphoreType.DMA((size, 2, count))
+    total = sum(b.size * 2 for b in blocks) * size
+    results = pl.pallas_call(
+        functools.partial(gather_kernel, size, count),
+        out_shape=shapes + shapes,
+        in_specs=[pl.BlockSpec(memory_space=pl.ANY)] * count,
+        out_specs=[pl.BlockSpec(memory_space=pl.ANY)] * (2 * count),
+        scratch_shapes=[sems, sems, sems, sems, pltpu.SemaphoreType.DMA((count,))],
+        compiler_params=pltpu.CompilerParams(collective_id=0, has_side_effects=True),
+        cost_estimate=pl.CostEstimate(flops=0, bytes_accessed=30 * total, transcendentals=0),
+    )(*blocks)
+    results = [r.reshape(-1, r.shape[-1]) for r in results]
+    return list(zip(results[:count], results[count:]))
+
+
+def scatter_kernel(size, groups, count, *refs):
+    mine, other = refs[:count], refs[count : 2 * count]
+    out, out_pair = refs[2 * count : 3 * count], refs[3 * count : 4 * count]
+    held, arrived = refs[4 * count : 5 * count], refs[5 * count : 6 * count]
+    sums = refs[6 * count : 7 * count]
+    pair_send, pair_recv, ring_send, ring_recv, rep_send, rep_recv, end_send, end_recv = refs[
+        7 * count :
+    ]
+    place = ring_place(size)
+    rep = lax.axis_index("rep")
+    core = lax.rem(rep, 2)
+    group = rep // 2
+    pair = sibling()
+    near = [{"shard": ring_member(place + 1, size)}, {"shard": ring_member(place - 1, size)}]
+    peers = [{"rep": 2 * lax.rem(group + d, groups) + core} for d in range(1, groups)]
+    greet(near + [pair] + peers)
+
+    def send(src, dst, send_sem, recv_sem, device):
+        copy = pltpu.make_async_remote_copy(
+            src_ref=src,
+            dst_ref=dst,
+            send_sem=send_sem,
+            recv_sem=recv_sem,
+            device_id=device,
+            device_id_type=MESH,
+        )
+        copy.start()
+        return copy
+
+    def owner(step, way):
+        return ring_member(place - 1 - step if way == 0 else place + 1 + step, size)
+
+    pairs, ring = {}, {}
+    for step in range(size):
+        for i in range(count):
+            for way in range(2):
+                index = owner(step, way)
+                at = (step, way, i)
+                pairs[at] = send(
+                    rows_of(other[i], index, way),
+                    rows_of(held[i], index, way),
+                    pair_send.at[at],
+                    pair_recv.at[at],
+                    pair,
+                )
+    for step in range(size):
+        for i in range(count):
+            rows = mine[i].shape[1] // 2
+            for way in range(2):
+                index = owner(step, way)
+                here = pl.ds(way * rows, rows)
+                at = (step, way, i)
+                pairs[at].wait_recv()
+                total = mine[i][index, here].astype(jnp.float32) + held[i][index, here].astype(
+                    jnp.float32
+                )
+                if step > 0:
+                    ring[step - 1, way, i].wait_recv()
+                    total = total + arrived[i][step - 1, here].astype(jnp.float32)
+                total = total.astype(jnp.bfloat16)
+                if step < size - 1:
+                    held[i][index, here] = total
+                    ring[at] = send(
+                        rows_of(held[i], index, way),
+                        rows_of(arrived[i], step, way),
+                        ring_send.at[at],
+                        ring_recv.at[at],
+                        near[way],
+                    )
+                else:
+                    sums[i][group, here] = total
+    reps = []
+    for i in range(count):
+        for d in range(1, groups):
+            reps.append(
+                send(
+                    sums[i].at[group],
+                    sums[i].at[group],
+                    rep_send.at[d, i],
+                    rep_recv.at[d, i],
+                    peers[d - 1],
+                )
+            )
+    for copy in reps:
+        copy.wait()
+    ends = []
+    for i in range(count):
+        total = sums[i][0].astype(jnp.float32)
+        for g in range(1, groups):
+            total = total + sums[i][g].astype(jnp.float32)
+        out[i][...] = total.astype(jnp.bfloat16)
+        ends.append(send(out[i], out_pair[i], end_send.at[i], end_recv.at[i], pair))
+    for copy in ends:
+        copy.wait()
+    for copy in ring.values():
+        copy.wait_send()
+    for copy in pairs.values():
+        copy.wait_send()
+
+
+def ring_scatter(mine, other, size, groups):
+    count = len(mine)
+    mine = [m.astype(jnp.bfloat16).reshape(size, -1, m.shape[-1]) for m in mine]
+    other = [m.astype(jnp.bfloat16).reshape(size, -1, m.shape[-1]) for m in other]
+    shapes = [jax.ShapeDtypeStruct(m.shape[1:], m.dtype) for m in mine]
+    vmem = pl.BlockSpec(memory_space=pltpu.VMEM)
+    sems = pltpu.SemaphoreType.DMA((size, 2, count))
+    rep_sems = pltpu.SemaphoreType.DMA((groups, count))
+    end_sems = pltpu.SemaphoreType.DMA((count,))
+    total = sum(m.size * 2 for m in mine)
+    results = pl.pallas_call(
+        functools.partial(scatter_kernel, size, groups, count),
+        out_shape=shapes + shapes,
+        in_specs=[vmem] * (2 * count),
+        out_specs=[vmem] * (2 * count),
+        scratch_shapes=[pltpu.VMEM(m.shape, m.dtype) for m in mine]
+        + [pltpu.VMEM((size - 1,) + m.shape[1:], m.dtype) for m in mine]
+        + [pltpu.VMEM((groups,) + m.shape[1:], m.dtype) for m in mine]
+        + [sems, sems, sems, sems, rep_sems, rep_sems, end_sems, end_sems],
+        compiler_params=pltpu.CompilerParams(
+            collective_id=1, has_side_effects=True, vmem_limit_bytes=48 * 1024 * 1024
+        ),
+        cost_estimate=pl.CostEstimate(flops=0, bytes_accessed=30 * total, transcendentals=0),
+    )(*mine, *other)
+    return list(zip(results[:count], results[count:]))
 
 
 def shards(
@@ -148,19 +383,28 @@
     key_heads = key_proj.shape[1] // head_size
     group_size = query_heads // key_heads
     length = tokens.shape[0]
-    gains = lax.all_gather(
-        jnp.concatenate([attn_gain, mlp_gain, query_gain, key_gain]), "shard", axis=0, tiled=False
-    ).astype(jnp.float32)
     step = width // size
     small = head_size // size
+    lanes = -(-2 * (step + small) // 128) * 128
+    gain_block = jnp.pad(
+        jnp.concatenate([attn_gain, mlp_gain, query_gain, key_gain]),
+        (0, lanes - 2 * (step + small)),
+    )
+    gain_pair, qkv, outs = ring_gather(
+        [
+            jnp.broadcast_to(gain_block[None], (32, lanes)),
+            jnp.concatenate(
+                [half_columns(w, core) for w in (query_proj, key_proj, value_proj)], axis=1
+            ),
+            half_columns(out_proj, core),
+        ],
+        size,
+    )
+    gains = gain_pair[0].reshape(size, 32, lanes)[:, 0].astype(jnp.float32)
     attn_scale = gains[:, :step].reshape(width)
     mlp_scale = gains[:, step : 2 * step].reshape(width)
     query_scale = gains[:, 2 * step : 2 * step + small].reshape(head_size)
-    key_scale = gains[:, 2 * step + small :].reshape(head_size)
-    qkv = gather_pair(
-        jnp.concatenate([half_columns(w, core) for w in (query_proj, key_proj, value_proj)], axis=1)
-    )
-    outs = gather_pair(half_columns(out_proj, core))
+    key_scale = gains[:, 2 * step + small : 2 * (step + small)].reshape(head_size)
     gate_up = gather_pair(
         jnp.concatenate([half_columns(w, core) for w in (gate_proj, up_proj)], axis=1)
     )
@@ -233,9 +477,7 @@
     grad_middle = cotangent.astype(jnp.float32) + norm_back(grad_inner, middle, inv_two, mlp_scale)
     grad_attn = grad_middle.astype(jnp.bfloat16)
     grad_attns = [half_columns(grad_attn, core), half_columns(grad_attn, 1 - core)]
-    out_part = scatter_pair(
-        left_product(mixed_b, grad_attns[0]), left_product(mixed_b, grad_attns[1])
-    )
+    out_grads = [left_product(mixed_b, g) for g in grad_attns]
     grad_mixed = (
         right_product(grad_attns[0], outs[0]) + right_product(grad_attns[1], outs[1])
     ).astype(jnp.bfloat16)
@@ -259,7 +501,7 @@
         jnp.concatenate([grad_query[:, :q_half], grad_key[:, :k_half], value_grad[:, :k_half]], 1),
         jnp.concatenate([grad_query[:, q_half:], grad_key[:, k_half:], value_grad[:, k_half:]], 1),
     ]
-    qkv_part = scatter_pair(left_product(normed, grad_qkv[0]), left_product(normed, grad_qkv[1]))
+    qkv_grads = [left_product(normed, g) for g in grad_qkv]
     grad_normed = right_product(grad_qkv[0], qkv[0]) + right_product(grad_qkv[1], qkv[1])
     attn_gain_grad = jnp.sum(grad_normed * inputs * inv_one, axis=0)
     tokens_grad = grad_middle + norm_back(grad_normed, inputs, inv_one, attn_scale)
@@ -273,13 +515,17 @@
         ],
         axis=1,
     )
-    gain_sums = lax.psum(gain_grads, ("rep", "shard"))
-    gain_sums = lax.dynamic_index_in_dim(
-        gain_sums, lax.axis_index("shard"), axis=0, keepdims=False
-    )
-
-    parts = [qkv_part, out_part, gate_up_part, down_part]
-    others = [from_sibling(p) for p in parts]
+    gain_grads = jnp.pad(gain_grads, ((0, 0), (0, lanes - gain_grads.shape[1])))
+    gain_grads = jnp.broadcast_to(gain_grads[:, None], (size, 32, lanes))
+    gain_pair, qkv_pair, out_pair = ring_scatter(
+        [gain_grads, qkv_grads[0], out_grads[0]],
+        [gain_grads, qkv_grads[1], out_grads[1]],
+        size,
+        lax.axis_size("rep") // 2,
+    )
+    gain_sums = gain_pair[0][0].astype(jnp.float32)
+    parts = [qkv_pair[0], out_pair[0], gate_up_part, down_part]
+    others = [qkv_pair[1], out_pair[1], from_sibling(gate_up_part), from_sibling(down_part)]
 
     def whole(index, start, stop):
         return in_order(
@@ -293,7 +539,7 @@
         tokens_grad,
         gain_sums[:step],
         gain_sums[2 * step : 2 * step + small],
-        gain_sums[2 * step + small :],
+        gain_sums[2 * step + small : 2 * (step + small)],
         whole(0, 0, q_half),
         whole(0, q_half, q_half + k_half),
         whole(0, q_half + k_half, q_half + 2 * k_half),

time: 966 us -> 664 us (0.69)
  waiting for transfers between devices: 521 us -> 35.2 us
  Pallas kernels: 0 us -> 257 us
  blocking collectives: 59 us -> 0 us
  matrix products: 159 us -> 138 us
  other arithmetic: 88.2 us -> 101 us
    pallas_call x0 -> x2, Pallas kernels: none -> 257 us  [the longest x1 139 us: ring_gather(): pl.pallas_call(functools.partial(gather_kernel, size, count), out_shape=s...]
    reduce_scatter x4 -> x2, waiting for transfers between devices: 235 us -> 0.01 us  [scatter_pair(): part = lax.psum_scatter(pair, 'shard', scatter_dimension=0, tiled=True)]
    all_gather x4 -> x2, waiting for transfers between devices: 226 us -> 0.02 us  [gather_pair(): mine = lax.all_gather(block, 'shard', axis=0, tiled=True)]
    psum x1 -> x0, blocking collectives: 39.5 us -> none  [shards(): gain_sums = lax.psum(gain_grads, ('rep', 'shard'))]
    unnamed x1 -> x0, blocking collectives: 19.5 us -> none
    ppermute x12 -> x6, waiting for transfers between devices: 15.7 us -> 0.02 us  [from_sibling(): return lax.ppermute(values, 'rep', sibling_pairs(lax.axis_size('rep')))]
    dot_general x8, matrix products: 41.1 us -> 28.2 us  [right_product(): lax.dot_general(left, right, (((1,), (1,)), ((), ())), preferred_element_...]
    unnamed x252 -> x216, local copies, waits for them, and re-layouts: 49.5 us -> 43.5 us
  transfers between devices with their start and end apart: 21 -> 11, of which waited for: 10 -> 1; matrix products, arithmetic and copies ran while one was open for 33% -> 49% of each run, Pallas kernels for 0% -> 39%
where the time goes in v2:
time: 664 us; the launch traced here: 653 us
  Pallas kernels  257 us (39%)
  matrix products  138 us (21%)
  local copies, waits for them, and re-layouts  104 us (16%)
  other arithmetic  101 us (15%)
  waiting for transfers between devices  35.2 us (5%)
  between operations  15.4 us (2%)
    pallas_call x1, Pallas kernels, ring_gather(): pl.pallas_call(functools.partial(gather_kernel, size, count), out_shape=s...  139 us
    pallas_call x1, Pallas kernels, ring_scatter(): pl.pallas_call(functools.partial(scatter_kernel, size, groups, count), ou...  118 us
    unnamed x216, local copies, waits for them, and re-layouts  43.5 us
    psum x1, waiting for transfers between devices, scatter_pair(): return lax.psum(part, 'rep', axis_index_groups=groups)  35 us
    dot_general x8, matrix products, left_product(): lax.dot_general(left, right, (((0,), (0,)), ((), ())), preferred_element_...  33.7 us
    dot_general x8, matrix products, product(): return jnp.dot(left, right, preferred_element_type=jnp.float32)  30.3 us
    dot_general x8, matrix products, right_product(): lax.dot_general(left, right, (((1,), (1,)), ((), ())), preferred_element_...  28.2 us
  transfers between devices with their start and end apart: 11, of which 1 were waited for; matrix products, arithmetic and copies ran while one was open for 49% of the time, Pallas kernels for 39%

profile of v2, /device:TPU:0, one launch (start us, length us, event | category | flops | bytes accessed | tf_op | source)
XLA Modules:
  0.0 652.7 jit_solution(17777603880657808985)
XLA Ops:
  12.9 139.3 %shard_map.228 = (bf16[8,32,384]{2,1,0:T(8,128)(2,1)}, bf16[8,128,2048]{2,1,0:T(8,128)(2,1)}, bf16[8,256,512]{2,1,0:T(8,128)(2,1)}, bf16[8,32,384]{2,1,0:T(8,128...) custom-call(bf16[32,384]{1,0:T(8,128)(2,1)} %broadcast_in_dim.12.refs_0_, ...), custom_call_target="tpu_custom_call" | custom-call | bytes 194641920 | tf_op jit(solution)/shard_map/pallas_call | solution.py:223
  190.4 5.4 copy.197
  214.0 5.4 copy.162
  222.0 5.4 copy.160
  245.3 7.5 %fusion.106 = (f32[8,2,512]{2,1,0:T(2,128)S(1)}, f32[8,2,512,512]{2,3,1,0:T(8,128)}) fusion(bf16[512,8,128,1]{0,2,3,1:T(8,128)(2,1)S(1)} %fusion.39, bf16[512,8,2,128]{0,3,2,1:T(8,128)(2,1)S(1)} %fusion.12, pred[512,512]{0,1:T(8,128)(4,1)S(1)} %iota_compare_fusion), kind=kOutput, calls=%fused_computation.249 | convolution fusion | flops 1086316544 | bytes 20217856 | tf_op jit(solution)/shard_map/qgjd,kgd->gjqk/dot_general | solution.py:62
  253.3 8.2 %fusion.3 = f32[8,2,512]{2,1,0:T(2,128)S(1)} fusion(f32[8,2,512,512]{2,3,1,0:T(8,128)} %get-tuple-element.170, f32[8,2,512]{2,1,0:T(2,128)S(1)} %get-tuple-element.169), kind=kLoop, calls=%fused_computation.9 | loop fusion | flops 8380416 | bytes 16842752 | tf_op jit(solution)/shard_map/reduce_sum | solution.py:73
  261.5 8.0 %fusion.35 = bf16[8,128,2,512]{3,1,2,0:T(8,128)(2,1)S(1)} fusion(f32[8,2,512,512]{2,3,1,0:T(8,128)} %get-tuple-element.170, f32[8,2,512]{2,1,0:T(2,128)S(1)} %fusion.3, f32[8,2,512]{2,1,0:T(2,128)S(1)} %get-tuple-element.169, bf16[512,4,128]{0,2,1:T(8,128)(2,1)S(1)} %bitcast.194, bf16[512,4,128]{0,2,1:T(8,128)(2,1)S(1)} %bitcast.196), kind=kOutput, calls=%fused_computation.105 | convolution fusion | flops 1089470464 | bytes 19988480 | tf_op jit(solution)/shard_map/gjqk,kgd->qgjd/dot_general | solution.py:75
  277.4 6.7 %fusion.107 = f32[512,3072]{1,0:T(8,128)S(1)} fusion(bf16[512,1024]{0,1:T(8,128)(2,1)} %multiply_convert_fusion.6, bf16[1024,3072]{1,0:T(8,128)(2,1)} %all-gather.3.cloned.1.call-done), kind=kOutput, calls=%fused_computation.250 | convolution fusion | flops 3221225472 | bytes 13631488 | tf_op jit(solution)/shard_map/dot_general | solution.py:15
  284.2 5.7 fusion.108
  308.8 5.5 convolution_convert_fusion
  314.5 5.6 add_convert_fusion.1
  320.2 6.7 %fusion.34 = f32[512,1024]{0,1:T(8,128)S(1)} fusion(bf16[1024,3072]{1,0:T(8,128)(2,1)} %all-gather.3.cloned.1.call-done, bf16[512,1536]{1,0:T(8,128)(2,1)} %get-tuple-element.103, bf16[512,1536]{1,0:T(8,128)(2,1)} %get-tuple-element.104), kind=kOutput, calls=%fused_computation.104 | convolution fusion | flops 3227516928 | bytes 11534336 | tf_op jit(solution)/shard_map/dot_general | solution.py:25
  326.9 6.9 %multiply_reduce_fusion.2 = (bf16[1024]{0:T(1024)(128)(2,1)S(1)}, f32[512]{0:T(512)S(1)}, f32[512,1024]{0,1:T(8,128)S(1)}) fusion(f32[512,1024]{0,1:T(8,128)S(1)} %get-tuple-element.98, f32[512]{0:T(512)S(1)} %get-tuple-element.164, f32[1024]{0:T(1024)S(1)} %get-tuple-element.157, f32[512,1024]{0,1:T(8,128)S(1)} %fusion.34, ...), kind=kOutput, calls=%fused_computation.93 | convolution fusion | flops 3231185408 | bytes 15738880 | tf_op jit(solution)/shard_map/dot_general | solution.py:25
  344.1 8.9 %bitcast_convert_fusion = bf16[8,128,512]{2,1,0:T(8,128)(2,1)S(1)} fusion(bf16[512,8,2,128]{0,3,2,1:T(8,128)(2,1)S(1)} %bitcast.170, f32[8,2,512,512]{2,3,1,0:T(8,128)} %get-tuple-element.170, f32[8,2,512]{2,1,0:T(2,128)S(1)} %bitcast.201), kind=kOutput, calls=%fused_computation.89 | convolution fusion | flops 1082654720 | bytes 19955712 | tf_op jit(solution)/shard_map/gjqk,qgjd->kgd/dot_general | solution.py:86
  356.1 11.8 %fusion = (f32[8,2,512]{2,1,0:T(2,128)S(1)}, f32[8,512,512,2]{2,1,3,0:T(8,128)}) fusion(f32[8,2,512,512]{2,3,1,0:T(8,128)} %get-tuple-element.170, f32[8,2,512]{2,1,0:T(2,128)S(1)} %bitcast.202, bf16[512,8,2,128]{0,3,2,1:T(8,128)(2,1)S(1)} %bitcast.171, bf16[512,4,128]{0,2,1:T(8,128)(2,1)S(1)} %bitcast.195, bf16[512,4,128]{0,2,1:T(8,128)(2,1)S(1)} %bitcast.197), kind=kOutput, calls=%fused_computation.2 | convolution fusion | flops 1088413696 | bytes 36765696 | tf_op jit(solution)/shard_map/qgjd,kgd->gjqk/dot_general | solution.py:83
  367.9 7.7 %add_convert_fusion = bf16[1024,3072]{1,0:T(8,128)(2,1)} fusion(bf16[1024,3072]{1,0:T(8,128)(2,1)} %collective-permute-done.2, bf16[512,1024]{0,1:T(8,128)(2,1)S(1)} %copy-done.30, bf16[512,1536]{1,0:T(8,128)(2,1)S(1)} %copy-done.59, bf16[512,1536]{1,0:T(8,128)(2,1)S(1)} %copy-done.60), kind=kOutput, calls=%fused_computation.11 | convolution fusion | flops 3236954112 | bytes 16777216 | tf_op jit(solution)/shard_map/dot_general | solution.py:19
  375.6 13.1 %fusion.2 = bf16[8,2,512,512]{2,3,1,0:T(8,128)(2,1)S(1)} fusion(f32[8,512,512,2]{2,1,3,0:T(8,128)} %get-tuple-element.173, f32[8,2,512,512]{2,3,1,0:T(8,128)} %get-tuple-element.170, f32[8,2,512]{2,1,0:T(2,128)S(1)} %get-tuple-element.172, f32[8,2,512]{2,1,0:T(2,128)S(1)} %bitcast.203), kind=kLoop, calls=%fused_computation.4 | loop fusion | flops 16777216 | bytes 42008576 | tf_op jit(solution)/shard_map/convert_element_type | solution.py:90
  397.6 6.7 %bitcast_multiply_fusion.6 = (f32[512,8,2,128]{0,3,2,1:T(8,128)S(1)}, f32[8,128,2,512]{3,1,2,0:T(8,128)}) fusion(bf16[512,8,128,1]{0,2,3,1:T(8,128)(2,1)S(1)} %copy-done.23, bf16[8,2,512,512]{2,3,1,0:T(8,128)(2,1)} %copy-done.2), kind=kOutput, calls=%fused_computation.46 | convolution fusion | flops 1074790400 | bytes 17825792 | tf_op jit(solution)/shard_map/gjqk,kgd->qgjd/dot_general | solution.py:91
  412.9 5.5 copy.161
  418.4 5.9 copy.200
  426.7 5.8 fusion.15
  436.6 7.3 %fusion.10 = bf16[512,2048]{1,0:T(8,128)(2,1)S(1)} fusion(f32[64,8,16,128]{3,2,1,0:T(8,128)S(1)} %bitcast.176, f32[64,8,16,128]{3,2,1,0:T(8,128)S(1)} %bitcast.177, f32[512,2048]{1,0:T(8,128)S(1)} %copy-done.18, f32[512,2048]{1,0:T(8,128)} %copy.161, f32[512,2048]{1,0:T(8,128)} %copy.200, f32[512,2048]{1,0:T(8,128)} %copy.160, f32[2048]{0:T(1024)S(1)} %copy-done.91, ...), kind=kLoop, calls=%fused_computation.27 | loop fusion | flops 9437184 | bytes 31465472 | tf_op jit(solution)/shard_map/convert_element_type | solution.py:496
  464.5 117.6 %shard_map.229 = (bf16[32,384]{1,0:T(8,128)(2,1)S(1)}, bf16[128,2048]{1,0:T(8,128)(2,1)S(1)}, bf16[256,512]{1,0:T(8,128)(2,1)S(1)}, bf16[32,384]{1,0:T(8,128)(2,...) custom-call(bf16[8,32,384]{2,1,0:T(8,128)(2,1)S(1)} %broadcast_in_dim.17.refs_0_.refs_3_, ...), custom_call_target="tpu_custom_call" | custom-call | bytes 194641920 | tf_op jit(solution)/shard_map/pallas_call | solution.py:346
  597.3 35.0 %all-reduce.5.cloned.1.call-done = (bf16[128,3072]{1,0:T(8,128)(2,1)}, bf16[384,512]{1,0:T(8,128)(2,1)}) async-done(((bf16[128,3072]{1,0:T(8,128)(2,1)}, bf16[384,512]{1,0:T(8,128)(2,1)}), (bf16[128,3072]{1,0:T(8,128)(2,1)}, bf16[384,512]{1,0:T(8,128)(2,1)})) %all-reduce.5.cloned.1.call-update) | async-done | bytes 1179664 | tf_op jit(solution)/shard_map/psum | solution.py:129
  (355 shorter events, 195.8 us)
Async XLA Ops:
  7.2 245.6 %all-gather.3.cloned.1.call-start = ((), (), s32[]{:S(2)}) async-start(), calls=%async_computation.2 | async-start | bytes 7077888 | tf_op jit(solution)/shard_map/all_gather | solution.py:119
  9.6 143.5 %copy-start.70 = (bf16[512,1024]{1,0:T(8,128)(2,1)S(1)}, bf16[512,1024]{1,0:T(8,128)(2,1)}, u32[]{:S(2)}) copy-start(bf16[512,1024]{1,0:T(8,128)(2,1)} %param.13) | copy-start | bytes 3145732
  9.7 267.6 %all-gather.5.cloned.1.call-start = ((), (), s32[]{:S(2)}) async-start(), calls=%async_computation.3 | async-start | bytes 3538944 | tf_op jit(solution)/shard_map/all_gather | solution.py:119
  10.5 577.6 %reduce-scatter.5.cloned.1.call-start = ((), (), s32[]{:S(2)}) async-start(), calls=%async_computation.5 | async-start | bytes 3538944 | tf_op jit(solution)/shard_map/reduce_scatter | solution.py:126
  168.0 69.7 %copy-start.6 = (f32[512,8,128]{0,2,1:T(8,128)}, f32[512,8,128]{0,2,1:T(8,128)S(1)}, u32[]{:S(2)}) copy-start(f32[512,8,128]{0,2,1:T(8,128)S(1)} %copy.147) | copy-start | bytes 6291460
  180.9 56.7 %copy-start.92 = (f32[128]{0:T(128)}, f32[128]{0:T(128)S(1)}, u32[]{:S(2)}) copy-start(f32[128]{0:T(128)S(1)} %mul.562) | copy-start | bytes 1540
  181.7 56.0 %copy-start.79 = (f32[512,8]{0,1:T(8,128)}, f32[512,8]{0,1:T(8,128)S(1)}, u32[]{:S(2)}) copy-start(f32[512,8]{0,1:T(8,128)S(1)} %get-tuple-element.156) | copy-start | bytes 49156
  185.5 54.6 %copy-start.35 = (f32[512,128]{0,1:T(8,128)}, f32[512,128]{0,1:T(8,128)S(1)}, u32[]{:S(2)}) copy-start(f32[512,128]{0,1:T(8,128)S(1)} %get-tuple-element.152) | copy-start | bytes 786436
  185.5 54.6 %copy-start.39 = (f32[512,128]{0,1:T(8,128)}, f32[512,128]{0,1:T(8,128)S(1)}, u32[]{:S(2)}) copy-start(f32[512,128]{0,1:T(8,128)S(1)} %get-tuple-element.151) | copy-start | bytes 786436
  198.6 41.5 %copy-start.82 = (f32[512,8,2]{0,2,1:T(2,128)}, f32[512,8,2]{0,2,1:T(2,128)S(1)}, u32[]{:S(2)}) copy-start(f32[512,8,2]{0,2,1:T(2,128)S(1)} %rsqrt.52) | copy-start | bytes 98308
  252.9 31.3 %collective-permute-start = (bf16[1024,3072]{1,0:T(8,128)(2,1)}, bf16[1024,3072]{1,0:T(8,128)(2,1)}, u32[]{:S(2)}, u32[]{:S(2)}) collective-permute-start(bf16[1024,3072]{1,0:T(8,128)(2,1)} %all-gather.3.cloned.1.call-done), channel_id=1, source_target_pairs={{0,8},{8,0},{16,24},{24,16},{1,9},{9,1},{17,25},{25,17},{2,10},{10... | collective-permute-start | bytes 18874376 | tf_op jit(solution)/shard_map/ppermute | solution.py:105
  275.3 58.5 %copy-start.11 = (f32[512,1024]{0,1:T(8,128)}, f32[512,1024]{0,1:T(8,128)S(1)}, u32[]{:S(2)}) copy-start(f32[512,1024]{0,1:T(8,128)S(1)} %get-tuple-element.98) | copy-start | bytes 6291460
  277.2 22.4 %collective-permute-start.1 = (bf16[3072,512]{1,0:T(8,128)(2,1)}, bf16[3072,512]{1,0:T(8,128)(2,1)}, u32[]{:S(2)}, u32[]{:S(2)}) collective-permute-start(bf16[3072,512]{1,0:T(8,128)(2,1)} %all-gather.5.cloned.1.call-done), channel_id=1, source_target_pairs={{0,8},{8,0},{16,24},{24,16},{1,9},{9,1},{17,25},{25,17},{2,10},{10... | collective-permute-start | bytes 9437192 | tf_op jit(solution)/shard_map/ppermute | solution.py:105
  297.5 17.0 %collective-permute-start.4 = (bf16[3072,512]{1,0:T(8,128)(2,1)}, bf16[3072,512]{1,0:T(8,128)(2,1)}, u32[]{:S(2)}, u32[]{:S(2)}) collective-permute-start(bf16[3072,512]{1,0:T(8,128)(2,1)} %convolution_convert_fusion.1), channel_id=1, source_target_pairs={{0,8},{8,0},{16,24},{24,16},{1,9},{9,1},{17,25},{25,17},{2,10},{10... | collective-permute-start | bytes 9437192 | tf_op jit(solution)/shard_map/ppermute | solution.py:105
  314.3 53.5 %collective-permute-start.2 = (bf16[1024,3072]{1,0:T(8,128)(2,1)}, bf16[1024,3072]{1,0:T(8,128)(2,1)}, u32[]{:S(2)}, u32[]{:S(2)}) collective-permute-start(bf16[1024,3072]{1,0:T(8,128)(2,1)} %convolution_convert_fusion), channel_id=1, source_target_pairs={{0,8},{8,0},{16,24},{24,16},{1,9},{9,1},{17,25},{25,17},{2,10},{10... | collective-permute-start | bytes 18874376 | tf_op jit(solution)/shard_map/ppermute | solution.py:105
  320.1 268.0 %reduce-scatter.3.cloned.1.call-start = ((), (), s32[]{:S(2)}) async-start(), calls=%async_computation.4 | async-start | bytes 7077888 | tf_op jit(solution)/shard_map/reduce_scatter | solution.py:126
  375.6 256.8 %all-reduce.5.cloned.1.call-start = ((), (), s32[]{:S(2)}) async-start(), calls=%async_computation.6 | async-start | bytes 2359296 | tf_op jit(solution)/shard_map/psum | solution.py:129
  375.6 13.1 %copy-start.14 = (bf16[512,8,2,128]{0,3,2,1:T(8,128)(2,1)S(1)}, bf16[512,8,2,128]{0,3,2,1:T(8,128)(2,1)}, u32[]{:S(2)}) copy-start(bf16[512,8,2,128]{0,3,2,1:T(8,128)(2,1)} %copy-done.13) | copy-start | bytes 6291460
  464.5 120.8 %copy-start.58 = (bf16[512,1536]{1,0:T(8,128)(2,1)S(1)}, bf16[512,1536]{1,0:T(8,128)(2,1)}, u32[]{:S(2)}) copy-start(bf16[512,1536]{1,0:T(8,128)(2,1)} %copy-done.56) | copy-start | bytes 4718596
  594.5 37.8 %copy-start.71 = (f32[128,512]{1,0:T(8,128)S(1)}, f32[128,512]{1,0:T(8,128)}, u32[]{:S(2)}) copy-start(f32[128,512]{1,0:T(8,128)} %get-tuple-element.136) | copy-start | bytes 786436
  594.5 37.8 %copy-start.72 = (f32[128,512]{1,0:T(8,128)S(1)}, f32[128,512]{1,0:T(8,128)}, u32[]{:S(2)}) copy-start(f32[128,512]{1,0:T(8,128)} %get-tuple-element.138) | copy-start | bytes 786436
  597.3 38.2 %copy-start.34 = (f32[512,1024]{0,1:T(8,128)S(1)}, f32[512,1024]{0,1:T(8,128)}, u32[]{:S(2)}) copy-start(f32[512,1024]{0,1:T(8,128)} %get-tuple-element.115) | copy-start | bytes 6291460
  632.3 8.3 %collective-permute-start.5 = (bf16[384,512]{1,0:T(8,128)(2,1)}, bf16[384,512]{1,0:T(8,128)(2,1)}, u32[]{:S(2)}, u32[]{:S(2)}) collective-permute-start(bf16[384,512]{1,0:T(8,128)(2,1)} %get-tuple-element.92), channel_id=1, source_target_pairs={{0,8},{8,0},{16,24},{24,16},{1,9},{9,1},{17,25},{25,17},{2,10},{10... | collective-permute-start | bytes 1179656 | tf_op jit(solution)/shard_map/ppermute | solution.py:105
  637.2 5.8 collective-permute-start.3
  (88 other events, 373.4 us)
Sparse Core Ops, SparseCore 0:
  10.8 145.4 all-gather.2
  159.1 59.5 all-gather.4
  320.2 74.6 reduce-scatter.4
  398.3 144.0 reduce-scatter.2
  588.3 44.0 all-reduce.4

commit v3 on v2

--- a/solution.py
+++ b/solution.py
@@ -123,10 +123,7 @@
 def scatter_pair(mine, other):
     received = from_sibling(other.astype(jnp.bfloat16))
     pair = (mine + received.astype(jnp.float32)).astype(jnp.bfloat16)
-    part = lax.psum_scatter(pair, "shard", scatter_dimension=0, tiled=True)
-    count = lax.axis_size("rep")
-    groups = [list(range(c, count, 2)) for c in range(2)]
-    return lax.psum(part, "rep", axis_index_groups=groups)
+    return lax.psum_scatter(pair, "shard", scatter_dimension=0, tiled=True)
 
 
 MESH = pl.DeviceIdType.MESH
@@ -233,14 +230,19 @@
     return list(zip(results[:count], results[count:]))
 
 
-def scatter_kernel(size, groups, count, *refs):
-    mine, other = refs[:count], refs[count : 2 * count]
-    out, out_pair = refs[2 * count : 3 * count], refs[3 * count : 4 * count]
-    held, arrived = refs[4 * count : 5 * count], refs[5 * count : 6 * count]
-    sums = refs[6 * count : 7 * count]
-    pair_send, pair_recv, ring_send, ring_recv, rep_send, rep_recv, end_send, end_recv = refs[
-        7 * count :
-    ]
+def scatter_kernel(size, groups, count, extra, *refs):
+    refs = list(refs)
+
+    def take(number):
+        taken = refs[:number]
+        del refs[:number]
+        return taken
+
+    every = count + extra
+    mine, other, parts = take(count), take(count), take(extra)
+    out, out_pair = take(every), take(every)
+    held, arrived, sums = take(count), take(count), take(every)
+    pair_send, pair_recv, ring_send, ring_recv, rep_send, rep_recv, end_send, end_recv = refs
     place = ring_place(size)
     rep = lax.axis_index("rep")
     core = lax.rem(rep, 2)
@@ -278,6 +280,23 @@
                     pair_recv.at[at],
                     pair,
                 )
+    reps = []
+
+    def exchange(i):
+        for d in range(1, groups):
+            reps.append(
+                send(
+                    sums[i].at[group],
+                    sums[i].at[group],
+                    rep_send.at[d, i],
+                    rep_recv.at[d, i],
+                    peers[d - 1],
+                )
+            )
+
+    for i in range(extra):
+        sums[count + i][group] = parts[i][...]
+        exchange(count + i)
     for step in range(size):
         for i in range(count):
             rows = mine[i].shape[1] // 2
@@ -304,22 +323,12 @@
                     )
                 else:
                     sums[i][group, here] = total
-    reps = []
     for i in range(count):
-        for d in range(1, groups):
-            reps.append(
-                send(
-                    sums[i].at[group],
-                    sums[i].at[group],
-                    rep_send.at[d, i],
-                    rep_recv.at[d, i],
-                    peers[d - 1],
-                )
-            )
+        exchange(i)
     for copy in reps:
         copy.wait()
     ends = []
-    for i in range(count):
+    for i in range(every):
         total = sums[i][0].astype(jnp.float32)
         for g in range(1, groups):
             total = total + sums[i][g].astype(jnp.float32)
@@ -333,31 +342,33 @@
         copy.wait_send()
 
 
-def ring_scatter(mine, other, size, groups):
-    count = len(mine)
+def ring_scatter(mine, other, parts, size, groups):
+    count, extra = len(mine), len(parts)
+    every = count + extra
     mine = [m.astype(jnp.bfloat16).reshape(size, -1, m.shape[-1]) for m in mine]
     other = [m.astype(jnp.bfloat16).reshape(size, -1, m.shape[-1]) for m in other]
     shapes = [jax.ShapeDtypeStruct(m.shape[1:], m.dtype) for m in mine]
+    shapes += [jax.ShapeDtypeStruct(p.shape, p.dtype) for p in parts]
     vmem = pl.BlockSpec(memory_space=pltpu.VMEM)
     sems = pltpu.SemaphoreType.DMA((size, 2, count))
-    rep_sems = pltpu.SemaphoreType.DMA((groups, count))
-    end_sems = pltpu.SemaphoreType.DMA((count,))
+    rep_sems = pltpu.SemaphoreType.DMA((groups, every))
+    end_sems = pltpu.SemaphoreType.DMA((every,))
     total = sum(m.size * 2 for m in mine)
     results = pl.pallas_call(
-        functools.partial(scatter_kernel, size, groups, count),
+        functools.partial(scatter_kernel, size, groups, count, extra),
         out_shape=shapes + shapes,
-        in_specs=[vmem] * (2 * count),
-        out_specs=[vmem] * (2 * count),
+        in_specs=[vmem] * (2 * count + extra),
+        out_specs=[vmem] * (2 * every),
         scratch_shapes=[pltpu.VMEM(m.shape, m.dtype) for m in mine]
         + [pltpu.VMEM((size - 1,) + m.shape[1:], m.dtype) for m in mine]
-        + [pltpu.VMEM((groups,) + m.shape[1:], m.dtype) for m in mine]
+        + [pltpu.VMEM((groups,) + shape.shape, shape.dtype) for shape in shapes]
         + [sems, sems, sems, sems, rep_sems, rep_sems, end_sems, end_sems],
         compiler_params=pltpu.CompilerParams(
             collective_id=1, has_side_effects=True, vmem_limit_bytes=48 * 1024 * 1024
         ),
         cost_estimate=pl.CostEstimate(flops=0, bytes_accessed=30 * total, transcendentals=0),
-    )(*mine, *other)
-    return list(zip(results[:count], results[count:]))
+    )(*mine, *other, *parts)
+    return list(zip(results[:every], results[every:]))
 
 
 def shards(
@@ -405,10 +416,12 @@
     mlp_scale = gains[:, step : 2 * step].reshape(width)
     query_scale = gains[:, 2 * step : 2 * step + small].reshape(head_size)
     key_scale = gains[:, 2 * step + small : 2 * (step + small)].reshape(head_size)
-    gate_up = gather_pair(
-        jnp.concatenate([half_columns(w, core) for w in (gate_proj, up_proj)], axis=1)
-    )
-    downs = gather_pair(half_columns(down_proj, core))
+    gate_up_block = jnp.concatenate([half_columns(w, core) for w in (gate_proj, up_proj)], axis=1)
+    gate_up_block, down_block, gains = lax.optimization_barrier(
+        (gate_up_block, half_columns(down_proj, core), gains)
+    )
+    gate_up = gather_pair(gate_up_block)
+    downs = gather_pair(down_block)
 
     q_half = query_proj.shape[1] // 2
     k_half = key_proj.shape[1] // 2
@@ -517,15 +530,16 @@
     )
     gain_grads = jnp.pad(gain_grads, ((0, 0), (0, lanes - gain_grads.shape[1])))
     gain_grads = jnp.broadcast_to(gain_grads[:, None], (size, 32, lanes))
-    gain_pair, qkv_pair, out_pair = ring_scatter(
+    gain_pair, qkv_pair, out_pair, gate_up_pair, down_pair = ring_scatter(
         [gain_grads, qkv_grads[0], out_grads[0]],
         [gain_grads, qkv_grads[1], out_grads[1]],
+        [gate_up_part, down_part],
         size,
         lax.axis_size("rep") // 2,
     )
     gain_sums = gain_pair[0][0].astype(jnp.float32)
-    parts = [qkv_pair[0], out_pair[0], gate_up_part, down_part]
-    others = [qkv_pair[1], out_pair[1], from_sibling(gate_up_part), from_sibling(down_part)]
+    pairs = [qkv_pair, out_pair, gate_up_pair, down_pair]
+    parts, others = zip(*pairs)
 
     def whole(index, start, stop):
         return in_order(

time: 664 us -> 610 us (0.919)
  Pallas kernels: 257 us -> 165 us
  waiting for transfers between devices: 35.2 us -> 69.2 us
    pallas_call x1, Pallas kernels: 139 us -> 69.3 us  [ring_gather(): pl.pallas_call(functools.partial(gather_kernel, size, count), out_shape=s...]
    all_gather x2, waiting for transfers between devices: 0.02 us -> 35.8 us  [gather_pair(): mine = lax.all_gather(block, 'shard', axis=0, tiled=True)]
    psum x1 -> x0, waiting for transfers between devices: 35 us -> none  [scatter_pair(): return lax.psum(part, 'rep', axis_index_groups=groups)]
    reduce_scatter x2, waiting for transfers between devices: 0.01 us -> 32.7 us  [scatter_pair(): return lax.psum_scatter(pair, 'shard', scatter_dimension=0, tiled=True)]
    pallas_call x1, Pallas kernels: 118 us -> 96.2 us  [ring_scatter(): pl.pallas_call(functools.partial(scatter_kernel, size, groups, count, ext...]
    unnamed x216 -> x210, local copies, waits for them, and re-layouts: 43.5 us -> 46.8 us
  transfers between devices with their start and end apart: 11 -> 8, of which waited for: 1 -> 2; matrix products, arithmetic and copies ran while one was open for 49% -> 51% of each run, Pallas kernels for 39% -> 0%
where the time goes in v3:
time: 610 us; the launch traced here: 598 us
  Pallas kernels  165 us (27%)
  matrix products  139 us (23%)
  local copies, waits for them, and re-layouts  109 us (18%)
  other arithmetic  99.4 us (16%)
  waiting for transfers between devices  69.2 us (11%)
  between operations  15.4 us (3%)
    pallas_call x1, Pallas kernels, ring_scatter(): pl.pallas_call(functools.partial(scatter_kernel, size, groups, count, ext...  96.2 us
    pallas_call x1, Pallas kernels, ring_gather(): pl.pallas_call(functools.partial(gather_kernel, size, count), out_shape=s...  69.3 us
    unnamed x210, local copies, waits for them, and re-layouts  46.8 us
    dot_general x8, matrix products, left_product(): lax.dot_general(left, right, (((0,), (0,)), ((), ())), preferred_element_...  38.1 us
    all_gather x2, waiting for transfers between devices, gather_pair(): mine = lax.all_gather(block, 'shard', axis=0, tiled=True)  35.8 us
    reduce_scatter x2, waiting for transfers between devices, scatter_pair(): return lax.psum_scatter(pair, 'shard', scatter_dimension=0, tiled=True)  32.7 us
    dot_general x8, matrix products, product(): return jnp.dot(left, right, preferred_element_type=jnp.float32)  28.3 us
    dot_general x8, matrix products, right_product(): lax.dot_general(left, right, (((1,), (1,)), ((), ())), preferred_element_...  26.8 us
  transfers between devices with their start and end apart: 8, of which 2 were waited for; matrix products, arithmetic and copies ran while one was open for 51% of the time, Pallas kernels for 0%

profile of v3, /device:TPU:0, one launch (start us, length us, event | category | flops | bytes accessed | tf_op | source)
XLA Modules:
  0.0 598.3 jit_solution(6033975767509955176)
XLA Ops:
  13.3 69.3 %shard_map.228 = (bf16[8,32,384]{2,1,0:T(8,128)(2,1)}, bf16[8,128,2048]{2,1,0:T(8,128)(2,1)}, bf16[8,256,512]{2,1,0:T(8,128)(2,1)}, bf16[8,32,384]{2,1,0:T(8,128...) custom-call(bf16[32,384]{1,0:T(8,128)(2,1)} %broadcast_in_dim.12.refs_0_, ...), custom_call_target="tpu_custom_call" | custom-call | bytes 194641920 | tf_op jit(solution)/shard_map/pallas_call | solution.py:220
  148.1 5.4 copy.162
  156.0 5.4 copy.160
  179.4 7.5 %fusion.106 = (f32[8,2,512]{2,1,0:T(2,128)S(1)}, f32[8,2,512,512]{2,3,1,0:T(8,128)}) fusion(bf16[512,8,128,1]{0,2,3,1:T(8,128)(2,1)S(1)} %fusion.39, bf16[512,8,2,128]{0,3,2,1:T(8,128)(2,1)S(1)} %fusion.12, pred[512,512]{0,1:T(8,128)(4,1)S(1)} %iota_compare_fusion), kind=kOutput, calls=%fused_computation.249 | convolution fusion | flops 1086316544 | bytes 20217856 | tf_op jit(solution)/shard_map/qgjd,kgd->gjqk/dot_general | solution.py:62
  187.4 8.2 %fusion.3 = f32[8,2,512]{2,1,0:T(2,128)S(1)} fusion(f32[8,2,512,512]{2,3,1,0:T(8,128)} %get-tuple-element.180, f32[8,2,512]{2,1,0:T(2,128)S(1)} %get-tuple-element.179), kind=kLoop, calls=%fused_computation.9 | loop fusion | flops 8380416 | bytes 16842752 | tf_op jit(solution)/shard_map/reduce_sum | solution.py:73
  195.7 8.1 %fusion.35 = bf16[8,128,2,512]{3,1,2,0:T(8,128)(2,1)S(1)} fusion(f32[8,2,512,512]{2,3,1,0:T(8,128)} %get-tuple-element.180, f32[8,2,512]{2,1,0:T(2,128)S(1)} %fusion.3, f32[8,2,512]{2,1,0:T(2,128)S(1)} %get-tuple-element.179, bf16[512,4,128]{0,2,1:T(8,128)(2,1)S(1)} %bitcast.192, bf16[512,4,128]{0,2,1:T(8,128)(2,1)S(1)} %bitcast.194), kind=kOutput, calls=%fused_computation.105 | convolution fusion | flops 1089470464 | bytes 19988480 | tf_op jit(solution)/shard_map/gjqk,kgd->qgjd/dot_general | solution.py:75
  211.4 35.7 %all-gather.5.cloned.1.call-done = bf16[3072,512]{1,0:T(8,128)(2,1)} async-done(((bf16[384,512]{1,0:T(8,128)(2,1)}), bf16[3072,512]{1,0:T(8,128)(2,1)}) %all-gather.5.cloned.1.call-update) | async-done | bytes 3145744 | tf_op jit(solution)/shard_map/all_gather | solution.py:119
  247.2 6.9 %fusion.107 = f32[512,3072]{1,0:T(8,128)S(1)} fusion(bf16[512,1024]{0,1:T(8,128)(2,1)} %multiply_convert_fusion.6, bf16[1024,3072]{1,0:T(8,128)(2,1)} %all-gather.3.cloned.1.call-done), kind=kOutput, calls=%fused_computation.250 | convolution fusion | flops 3221225472 | bytes 13631488 | tf_op jit(solution)/shard_map/dot_general | solution.py:15
  254.1 5.7 fusion.108
  278.3 5.5 convolution_convert_fusion
  284.3 5.4 add_convert_fusion.1
  289.9 6.7 %fusion.34 = f32[512,1024]{0,1:T(8,128)S(1)} fusion(bf16[1024,3072]{1,0:T(8,128)(2,1)} %all-gather.3.cloned.1.call-done, bf16[512,1536]{1,0:T(8,128)(2,1)} %get-tuple-element.113, bf16[512,1536]{1,0:T(8,128)(2,1)} %get-tuple-element.114), kind=kOutput, calls=%fused_computation.104 | convolution fusion | flops 3227516928 | bytes 11534336 | tf_op jit(solution)/shard_map/dot_general | solution.py:25
  296.6 6.7 %multiply_reduce_fusion.2 = (bf16[1024]{0:T(1024)(128)(2,1)S(1)}, f32[512]{0:T(512)S(1)}, f32[512,1024]{0,1:T(8,128)S(1)}) fusion(f32[512,1024]{0,1:T(8,128)S(1)} %get-tuple-element.108, f32[512]{0:T(512)S(1)} %get-tuple-element.174, f32[1024]{0:T(1024)S(1)} %get-tuple-element.167, f32[512,1024]{0,1:T(8,128)S(1)} %fusion.34, ...), kind=kOutput, calls=%fused_computation.93 | convolution fusion | flops 3231185408 | bytes 15738880 | tf_op jit(solution)/shard_map/dot_general | solution.py:25
  313.6 8.8 %bitcast_convert_fusion = bf16[8,128,512]{2,1,0:T(8,128)(2,1)S(1)} fusion(bf16[512,8,2,128]{0,3,2,1:T(8,128)(2,1)S(1)} %bitcast.168, f32[8,2,512,512]{2,3,1,0:T(8,128)} %get-tuple-element.180, f32[8,2,512]{2,1,0:T(2,128)S(1)} %bitcast.201), kind=kOutput, calls=%fused_computation.89 | convolution fusion | flops 1082654720 | bytes 19955712 | tf_op jit(solution)/shard_map/gjqk,qgjd->kgd/dot_general | solution.py:86
  325.5 11.6 %fusion = (f32[8,2,512]{2,1,0:T(2,128)S(1)}, f32[8,512,512,2]{2,1,3,0:T(8,128)}) fusion(f32[8,2,512,512]{2,3,1,0:T(8,128)} %get-tuple-element.180, f32[8,2,512]{2,1,0:T(2,128)S(1)} %bitcast.202, bf16[512,8,2,128]{0,3,2,1:T(8,128)(2,1)S(1)} %bitcast.169, bf16[512,4,128]{0,2,1:T(8,128)(2,1)S(1)} %bitcast.193, bf16[512,4,128]{0,2,1:T(8,128)(2,1)S(1)} %bitcast.195), kind=kOutput, calls=%fused_computation.2 | convolution fusion | flops 1088413696 | bytes 36765696 | tf_op jit(solution)/shard_map/qgjd,kgd->gjqk/dot_general | solution.py:83
  337.2 7.7 %add_convert_fusion = bf16[1024,3072]{1,0:T(8,128)(2,1)} fusion(bf16[1024,3072]{1,0:T(8,128)(2,1)} %collective-permute-done.2, bf16[512,1024]{0,1:T(8,128)(2,1)S(1)} %copy-done.33, bf16[512,1536]{1,0:T(8,128)(2,1)S(1)} %copy-done.59, bf16[512,1536]{1,0:T(8,128)(2,1)S(1)} %copy-done.60), kind=kOutput, calls=%fused_computation.11 | convolution fusion | flops 3236954112 | bytes 16777216 | tf_op jit(solution)/shard_map/dot_general | solution.py:19
  345.0 13.1 %fusion.2 = bf16[8,2,512,512]{2,3,1,0:T(8,128)(2,1)S(1)} fusion(f32[8,512,512,2]{2,1,3,0:T(8,128)} %get-tuple-element.183, f32[8,2,512,512]{2,3,1,0:T(8,128)} %get-tuple-element.180, f32[8,2,512]{2,1,0:T(2,128)S(1)} %get-tuple-element.182, f32[8,2,512]{2,1,0:T(2,128)S(1)} %bitcast.203), kind=kLoop, calls=%fused_computation.4 | loop fusion | flops 16777216 | bytes 42008576 | tf_op jit(solution)/shard_map/convert_element_type | solution.py:90
  366.2 6.6 %bitcast_multiply_fusion.6 = (f32[512,8,2,128]{0,3,2,1:T(8,128)S(1)}, f32[8,128,2,512]{3,1,2,0:T(8,128)}) fusion(bf16[512,8,128,1]{0,2,3,1:T(8,128)(2,1)S(1)} %copy-done.26, bf16[8,2,512,512]{2,3,1,0:T(8,128)(2,1)} %copy-done.4), kind=kOutput, calls=%fused_computation.46 | convolution fusion | flops 1074790400 | bytes 17825792 | tf_op jit(solution)/shard_map/gjqk,kgd->qgjd/dot_general | solution.py:91
  382.0 5.4 copy.161
  387.3 5.8 copy.200
  399.1 7.5 %fusion.10 = bf16[512,2048]{1,0:T(8,128)(2,1)S(1)} fusion(f32[64,8,16,128]{3,2,1,0:T(8,128)S(1)} %bitcast.174, f32[64,8,16,128]{3,2,1,0:T(8,128)S(1)} %bitcast.175, f32[512,2048]{1,0:T(8,128)S(1)} %copy-done.21, f32[512,2048]{1,0:T(8,128)} %copy.161, f32[512,2048]{1,0:T(8,128)} %copy.200, f32[512,2048]{1,0:T(8,128)} %copy.160, f32[2048]{0:T(1024)S(1)} %copy-done.92, ...), kind=kLoop, calls=%fused_computation.27 | loop fusion | flops 9437184 | bytes 31465472 | tf_op jit(solution)/shard_map/convert_element_type | solution.py:509
  428.3 6.5 %fusion.15 = bf16[128]{0:T(256)(128)(2,1)S(1)} fusion(f32[512,8,2,128]{0,3,2,1:T(8,128)} %bitcast.177, f32[512,8,2,64]{0,3,2,1:T(8,128)} %bitcast.171, f32[512,8,2,64]{0,3,2,1:T(8,128)} %bitcast.170, f32[8,128,2,512]{3,1,2,0:T(8,128)} %get-tuple-element.187, f32[512,128]{0,1:T(8,128)S(1)} %copy-done.45, f32[512,8,2]{0,2,1:T(2,128)S(1)} %copy-done.87), kind=kLoop, calls=%fused_computation.37 | loop fusion | flops 6291328 | bytes 12878080 | tf_op jit(solution)/shard_map/reduce_sum | solution.py:506
  450.9 32.7 %reduce-scatter.3.cloned.1.call-done.refs_6_ = bf16[128,3072]{1,0:T(8,128)(2,1)} async-done(((bf16[1024,3072]{1,0:T(8,128)(2,1)}), bf16[128,3072]{1,0:T(8,128)(2,1)}) %reduce-scatter.3.cloned.1.call-update) | async-done | bytes 786448 | tf_op jit(solution)/shard_map/reduce_scatter | solution.py:126
  485.7 96.2 %shard_map.229 = (bf16[32,384]{1,0:T(8,128)(2,1)S(1)}, bf16[128,2048]{1,0:T(8,128)(2,1)S(1)}, bf16[256,512]{1,0:T(8,128)(2,1)S(1)}, bf16[128,3072]{1,0:T(8,128)(...) custom-call(bf16[8,32,384]{2,1,0:T(8,128)(2,1)S(1)} %broadcast_in_di, ...), custom_call_target="tpu_custom_call" | custom-call | bytes 194641920 | tf_op jit(solution)/shard_map/pallas_call | solution.py:357
  (342 shorter events, 204.4 us)
Async XLA Ops:
  7.2 76.3 %copy-start = (bf16[384,1024]{1,0:T(8,128)(2,1)S(1)}, bf16[384,1024]{1,0:T(8,128)(2,1)}, u32[]{:S(2)}) copy-start(bf16[384,1024]{1,0:T(8,128)(2,1)} %param.25) | copy-start | bytes 2359300
  7.2 77.1 %copy-start.88 = (bf16[128,3072]{1,0:T(8,128)(2,1)S(1)}, bf16[128,3072]{1,0:T(8,128)(2,1)}, u32[]{:S(2)}) copy-start(bf16[128,3072]{1,0:T(8,128)(2,1)} %param.24) | copy-start | bytes 2359300
  7.2 179.7 %all-gather.3.cloned.1.call-start = ((), (), s32[]{:S(2)}) async-start(), calls=%async_computation.2 | async-start | bytes 7077888 | tf_op jit(solution)/shard_map/all_gather | solution.py:119
  11.9 75.4 %copy-start.70 = (bf16[512,1024]{1,0:T(8,128)(2,1)S(1)}, bf16[512,1024]{1,0:T(8,128)(2,1)}, u32[]{:S(2)}) copy-start(bf16[512,1024]{1,0:T(8,128)(2,1)} %param.13) | copy-start | bytes 3145732
  86.3 160.8 %all-gather.5.cloned.1.call-start = ((), (), s32[]{:S(2)}) async-start(), calls=%async_computation.3 | async-start | bytes 3538944 | tf_op jit(solution)/shard_map/all_gather | solution.py:119
  87.1 363.8 %reduce-scatter.5.cloned.1.call-start = ((), (), s32[]{:S(2)}) async-start(), calls=%async_computation.5 | async-start | bytes 3538944 | tf_op jit(solution)/shard_map/reduce_scatter | solution.py:126
  102.0 69.7 %copy-start.8 = (f32[512,8,128]{0,2,1:T(8,128)}, f32[512,8,128]{0,2,1:T(8,128)S(1)}, u32[]{:S(2)}) copy-start(f32[512,8,128]{0,2,1:T(8,128)S(1)} %copy.147) | copy-start | bytes 6291460
  115.0 56.7 %copy-start.93 = (f32[128]{0:T(128)}, f32[128]{0:T(128)S(1)}, u32[]{:S(2)}) copy-start(f32[128]{0:T(128)S(1)} %mul.562) | copy-start | bytes 1540
  115.7 56.0 %copy-start.84 = (f32[512,8]{0,1:T(8,128)}, f32[512,8]{0,1:T(8,128)S(1)}, u32[]{:S(2)}) copy-start(f32[512,8]{0,1:T(8,128)S(1)} %get-tuple-element.166) | copy-start | bytes 49156
  119.5 54.6 %copy-start.37 = (f32[512,128]{0,1:T(8,128)}, f32[512,128]{0,1:T(8,128)S(1)}, u32[]{:S(2)}) copy-start(f32[512,128]{0,1:T(8,128)S(1)} %get-tuple-element.162) | copy-start | bytes 786436
  119.5 54.7 %copy-start.41 = (f32[512,128]{0,1:T(8,128)}, f32[512,128]{0,1:T(8,128)S(1)}, u32[]{:S(2)}) copy-start(f32[512,128]{0,1:T(8,128)S(1)} %get-tuple-element.161) | copy-start | bytes 786436
  132.8 41.4 %copy-start.86 = (f32[512,8,2]{0,2,1:T(2,128)}, f32[512,8,2]{0,2,1:T(2,128)S(1)}, u32[]{:S(2)}) copy-start(f32[512,8,2]{0,2,1:T(2,128)S(1)} %rsqrt.52) | copy-start | bytes 98308
  186.9 67.1 %collective-permute-start = (bf16[1024,3072]{1,0:T(8,128)(2,1)}, bf16[1024,3072]{1,0:T(8,128)(2,1)}, u32[]{:S(2)}, u32[]{:S(2)}) collective-permute-start(bf16[1024,3072]{1,0:T(8,128)(2,1)} %all-gather.3.cloned.1.call-done), channel_id=1, source_target_pairs={{0,8},{8,0},{16,24},{24,16},{1,9},{9,1},{17,25},{25,17},{2,10},{10... | collective-permute-start | bytes 18874376 | tf_op jit(solution)/shard_map/ppermute | solution.py:105
  187.4 8.3 %copy-start.49 = (bf16[512,512]{0,1:T(8,128)(2,1)S(1)}, bf16[512,512]{0,1:T(8,128)(2,1)}, u32[]{:S(2)}) copy-start(bf16[512,512]{0,1:T(8,128)(2,1)} %copy.193) | copy-start | bytes 1572868
  209.5 93.8 %copy-start.13 = (f32[512,1024]{0,1:T(8,128)}, f32[512,1024]{0,1:T(8,128)S(1)}, u32[]{:S(2)}) copy-start(f32[512,1024]{0,1:T(8,128)S(1)} %get-tuple-element.108) | copy-start | bytes 6291460
  247.2 22.0 %collective-permute-start.1 = (bf16[3072,512]{1,0:T(8,128)(2,1)}, bf16[3072,512]{1,0:T(8,128)(2,1)}, u32[]{:S(2)}, u32[]{:S(2)}) collective-permute-start(bf16[3072,512]{1,0:T(8,128)(2,1)} %all-gather.5.cloned.1.call-done), channel_id=1, source_target_pairs={{0,8},{8,0},{16,24},{24,16},{1,9},{9,1},{17,25},{25,17},{2,10},{10... | collective-permute-start | bytes 9437192 | tf_op jit(solution)/shard_map/ppermute | solution.py:105
  267.3 17.0 %collective-permute-start.3 = (bf16[3072,512]{1,0:T(8,128)(2,1)}, bf16[3072,512]{1,0:T(8,128)(2,1)}, u32[]{:S(2)}, u32[]{:S(2)}) collective-permute-start(bf16[3072,512]{1,0:T(8,128)(2,1)} %convolution_convert_fusion.1), channel_id=1, source_target_pairs={{0,8},{8,0},{16,24},{24,16},{1,9},{9,1},{17,25},{25,17},{2,10},{10... | collective-permute-start | bytes 9437192 | tf_op jit(solution)/shard_map/ppermute | solution.py:105
  283.8 53.3 %collective-permute-start.2 = (bf16[1024,3072]{1,0:T(8,128)(2,1)}, bf16[1024,3072]{1,0:T(8,128)(2,1)}, u32[]{:S(2)}, u32[]{:S(2)}) collective-permute-start(bf16[1024,3072]{1,0:T(8,128)(2,1)} %convolution_convert_fusion), channel_id=1, source_target_pairs={{0,8},{8,0},{16,24},{24,16},{1,9},{9,1},{17,25},{25,17},{2,10},{10... | collective-permute-start | bytes 18874376 | tf_op jit(solution)/shard_map/ppermute | solution.py:105
  289.8 193.8 %reduce-scatter.3.cloned.1.call-start = ((), (), s32[]{:S(2)}) async-start(), calls=%async_computation.4 | async-start | bytes 7077888 | tf_op jit(solution)/shard_map/reduce_scatter | solution.py:126
  325.5 11.6 %copy-start.33 = (bf16[512,1024]{0,1:T(8,128)(2,1)S(1)}, bf16[512,1024]{0,1:T(8,128)(2,1)}, u32[]{:S(2)}) copy-start(bf16[512,1024]{0,1:T(8,128)(2,1)} %multiply_convert_fusion.6) | copy-start | bytes 3145732
  325.5 11.6 %copy-start.59 = (bf16[512,1536]{1,0:T(8,128)(2,1)S(1)}, bf16[512,1536]{1,0:T(8,128)(2,1)}, u32[]{:S(2)}) copy-start(bf16[512,1536]{1,0:T(8,128)(2,1)} %get-tuple-element.113) | copy-start | bytes 4718596
  325.5 11.7 %copy-start.60 = (bf16[512,1536]{1,0:T(8,128)(2,1)S(1)}, bf16[512,1536]{1,0:T(8,128)(2,1)}, u32[]{:S(2)}) copy-start(bf16[512,1536]{1,0:T(8,128)(2,1)} %get-tuple-element.114) | copy-start | bytes 4718596
  344.9 13.2 %copy-start.16 = (bf16[512,8,2,128]{0,3,2,1:T(8,128)(2,1)S(1)}, bf16[512,8,2,128]{0,3,2,1:T(8,128)(2,1)}, u32[]{:S(2)}) copy-start(bf16[512,8,2,128]{0,3,2,1:T(8,128)(2,1)} %copy-done.15) | copy-start | bytes 6291460
  344.9 13.2 %copy-start.46 = (f32[512,128]{0,1:T(8,128)S(1)}, f32[512,128]{0,1:T(8,128)}, u32[]{:S(2)}) copy-start(f32[512,128]{0,1:T(8,128)} %get-tuple-element.160) | copy-start | bytes 786436
  (82 other events, 311.5 us)
Sparse Core Ops, SparseCore 0:
  86.5 99.2 all-gather.2
  188.5 58.6 all-gather.4
  289.9 73.1 reduce-scatter.4
  366.5 116.9 reduce-scatter.2
